TPU v7x, 256 devices: a whole 4x4x8 slice. The times are simulated.
256 devices in a mesh: band: 64 (over x, z, core), lev: 4 (over y).
Axes of the slice: x: 4, y: 4, z: 8, core: 2. Of those that a mesh axis runs over, the one named last changes fastest.
Arguments:
- jacobian: bfloat16 [20480, 13824], P('band', 'lev'), may hold values from -0.375 to 0.375
- departures: bfloat16 [20480, 256], P('band', 'lev'), may hold values from -6 to 6
- level_index: int32 [20480, 54], P('band'), may hold values from 0 to 134
- level_weight: bfloat16 [20480, 54], P('band'), may hold values from 0 to 1
- column_index: int32 [20480], P('band'), may hold values from 0 to 344063, as said below
- record_counts: int32 [4096], P('band'), may hold values from 0 to 5, as said below
Outputs:
- spectra: bfloat16 [136, 128, 2560], P('lev', None, 'band')
Inputs may be any that keep to these rules, and one draw needn't show every extreme that they name: `column_index`: record i goes to band b = (i // 5) mod (number of bands) and its column lies in that band's rows: b * 2 * 2688 <= column < (b + 1) * 2 * 2688. `record_counts`: entry s * (number of bands) + b counts the live slots, the first ones, among the 5 slots that reader s fills for band b; in every draw some band receives 5 live records from every reader.
All inputs are finite; a program needn't handle non-finite values.
Results may differ from a plain program's by a relative error of at most 0.0055.
Values may be sent and summed in bfloat16 or wider, within the bound.
No kernel may reach another device: no remote copies, remote signals or barrier semaphores. Data moves between devices by JAX's collectives and lax.ppermute only.
A program may use at most 128 MiB of HBM per device.

v0:
```python
import math

import jax
import jax.numpy as jnp
from jax import lax
from jax.sharding import PartitionSpec as P

KL = 54
LEVELS = 136
NLON = 2688
NM = 1280
ROWS = 2


def dft_table():
    longitude = jnp.arange(NLON, dtype=jnp.int32)[:, None]
    wavenumber = jnp.arange(NM, dtype=jnp.int32)[None, :]
    phase_index = longitude * wavenumber % NLON
    angles = phase_index.astype(jnp.float32) * (2.0 * math.pi / NLON)
    stacked = jnp.stack([jnp.cos(angles), -jnp.sin(angles)], axis=2)
    return stacked.reshape(NLON, 2 * NM).astype(jnp.bfloat16)


def profiles(contrib, level_index, level_weight, record_total):
    weights = level_weight.astype(jnp.float32)
    row_offset = (jnp.arange(record_total, dtype=jnp.int32) * LEVELS)[:, None]
    lower_ids = (row_offset + level_index).reshape(-1)
    lower_terms = (contrib * (1.0 - weights)).reshape(-1)
    upper_terms = (contrib * weights).reshape(-1)
    summed = jax.ops.segment_sum(lower_terms, lower_ids, num_segments=record_total * LEVELS)
    summed = summed + jax.ops.segment_sum(
        upper_terms, lower_ids + 1, num_segments=record_total * LEVELS
    )
    return summed.reshape(record_total, LEVELS)


def contract_rows(jacobian_rows, departure_rows, counts_rows, capacity):
    record_total = jacobian_rows.shape[0]
    channels = departure_rows.shape[1]
    contrib = jnp.einsum(
        "ock,oc->ok",
        jacobian_rows.reshape(record_total, channels, KL),
        departure_rows,
        preferred_element_type=jnp.float32,
    )
    record_ids = jnp.arange(record_total, dtype=jnp.int32)
    usable = record_ids % capacity < counts_rows[record_ids // capacity]
    return jnp.where(usable[:, None], contrib, jnp.zeros_like(contrib))


def local(jacobian, departures, level_index, level_weight, column_index, record_counts):
    owners = lax.axis_size("band")
    cols_dev = ROWS * NLON
    level_share = LEVELS // lax.axis_size("lev")
    jacobian_in, departure_in, index_in, weight_in, column_in, counts_in = (
        lax.all_to_all(jacobian, "band", split_axis=0, concat_axis=0, tiled=True),
        lax.all_to_all(departures, "band", split_axis=0, concat_axis=0, tiled=True),
        lax.all_to_all(level_index, "band", split_axis=0, concat_axis=0, tiled=True),
        lax.all_to_all(level_weight, "band", split_axis=0, concat_axis=0, tiled=True),
        lax.all_to_all(column_index, "band", split_axis=0, concat_axis=0, tiled=True),
        lax.all_to_all(record_counts, "band", split_axis=0, concat_axis=0, tiled=True),
    )
    record_total = jacobian_in.shape[0]
    capacity = record_total // owners
    contrib = contract_rows(jacobian_in, departure_in, counts_in, capacity)
    local_column = column_in - lax.axis_index("band") * cols_dev
    profile = profiles(contrib, index_in, weight_in, record_total)
    gridded = jnp.zeros((LEVELS, cols_dev), jnp.float32).at[:, local_column].add(profile.T)
    increment_sum = lax.psum_scatter(gridded, "lev", scatter_dimension=0, tiled=True)
    increments = increment_sum.astype(jnp.bfloat16).reshape(level_share * ROWS, NLON)
    spectra = jnp.dot(increments, dft_table(), preferred_element_type=jnp.float32).astype(
        jnp.bfloat16
    )
    spectra = spectra.reshape(level_share, ROWS, 2 * NM)
    return lax.all_to_all(spectra, "band", split_axis=2, concat_axis=1, tiled=True)


def solution(mesh):
    placed = (
        P("band", "lev"),
        P("band", "lev"),
        P("band", None),
        P("band", None),
        P("band"),
        P("band"),
    )
    return jax.shard_map(
        local, mesh=mesh, in_specs=placed, out_specs=P("lev", None, "band"), check_vma=False
    )
```

profile of v0, /device:TPU:1, one launch (start us, length us, event | category | flops | bytes accessed | tf_op | source)
XLA Modules:
  0.0 742.0 jit_solution(13220340872165080618)
XLA Ops:
  1.4 13.0 %all-to-all-start.2 = ((s32[64,1,1]{2,1,0:T(1,128)}), s32[64,1,1]{2,1,0:T(1,128)S(1)}, u32[]{:S(2)}, u32[]{:S(2)}) async-start(s32[64,1,1]{2,1,0:T(1,128)} %copy.36), calls=%async_computation.2 | async-start | bytes 65536 | tf_op jit(solution)/shard_map/all_to_all | solution.py:61
  26.4 60.1 %negate_convert_fusion = (bf16[2688,1280,1]{1,0,2:T(8,128)(2,1)}, bf16[2688,1280,1]{1,0,2:T(8,128)(2,1)}) fusion(), kind=kLoop, calls=%fused_computation.6 | loop fusion | flops 41287680 | bytes 13762560 | tf_op jit(solution)/shard_map/convert.2
  89.1 12.8 %pad_maximum_fusion = bf16[2688,1280,2]{1,0,2:T(8,128)(2,1)} fusion(bf16[2688,1280,1]{1,0,2:T(8,128)(2,1)} %get-tuple-element.73, bf16[2688,1280,1]{1,0,2:T(8,128)(2,1)} %get-tuple-element.74), kind=kLoop, calls=%fused_computation.5 | loop fusion | flops 6881280 | bytes 27525120 | tf_op jit(solution)/shard_map/stack | solution.py:20
  103.9 2.6 all_to_all.63
  106.5 35.8 %copy.40 = bf16[2688,1280,2]{0,2,1:T(2,128)(2,1)} copy(bf16[2688,1280,2]{1,0,2:T(8,128)(2,1)} %pad_maximum_fusion) | data formatting | bytes 27525120 | tf_op jit(solution)/shard_map/stack | solution.py:20
  142.2 27.9 %convert_element_type.42 = bf16[2688,2560]{0,1:T(8,128)(2,1)} reshape(bf16[2688,1280,2]{0,2,1:T(2,128)(2,1)} %copy.40) | data formatting | bytes 27525120 | tf_op jit(solution)/shard_map/convert_element_type | solution.py:21
  170.1 10.3 %all-to-all-start = ((s32[64,5,1]{1,2,0:T(1,128)}), s32[64,5,1]{1,2,0:T(1,128)S(1)}, u32[]{:S(2)}, u32[]{:S(2)}) async-start(s32[64,5,1]{1,2,0:T(1,128)} %bitcast), calls=%async_computation | async-start | bytes 65536 | tf_op jit(solution)/shard_map/all_to_all | solution.py:60
  182.4 7.4 all-to-all-done
  190.4 4.7 all-to-all-start.5
  214.4 10.4 %all-to-all-start.4 = ((bf16[64,2,160]{2,1,0:T(2,128)(2,1)}), bf16[64,2,160]{2,1,0:T(2,128)(2,1)S(1)}, u32[]{:S(2)}, u32[]{:S(2)}) async-start(bf16[64,2,160]{2,1,0:T(2,128)(2,1)} %reshape.654), calls=%async_computation.4 | async-start | bytes 131072 | tf_op jit(solution)/shard_map/all_to_all | solution.py:57
  225.5 9.1 %all-to-all-done.4 = bf16[64,2,160]{2,1,0:T(2,128)(2,1)S(1)} async-done(((bf16[64,2,160]{2,1,0:T(2,128)(2,1)}), bf16[64,2,160]{2,1,0:T(2,128)(2,1)S(1)}, u32[]{:S(2)}, u32[]{:S(2)}) %all-to-all-start.4) | async-done | bytes 40992 | tf_op jit(solution)/shard_map/all_to_all | solution.py:57
  235.3 4.5 all-to-all-start.1
  241.1 9.0 %all-to-all-done.1 = s32[64,1,270]{2,1,0:T(1,128)S(1)} async-done(((s32[64,1,270]{2,1,0:T(1,128)}), s32[64,1,270]{2,1,0:T(1,128)S(1)}, u32[]{:S(2)}, u32[]{:S(2)}) %all-to-all-start.1) | async-done | bytes 69152 | tf_op jit(solution)/shard_map/all_to_all | solution.py:58
  250.7 4.6 all-to-all-start.3
  256.6 4.4 fusion.13
  260.9 37.5 %fusion.9 = pred[320]{0:T(512)(128)(4,1)S(1)} fusion(pred[320]{0:T(512)(128)(4,1)} %compare_reduce_fusion, pred[320]{0:T(512)(128)(4,1)} %compare_reduce_fusion.1, pred[320]{0:T(512)(128)(4,1)} %compare_reduce_fusion.2, pred[320]{0:T(512)(128)(4,1)} %compare_reduce_fusion.3, pred[320]{0:T(512)(128)(4,1)} %compare_reduce_fusion.4, ...), kind=kLoop, calls=%fused_computation.92 | loop fusion | flops 20480 | bytes 20068 | tf_op jit(solution)/shard_map/lt | solution.py:47
  315.7 21.6 %all-to-all-done.3 = bf16[64,5,3456]{2,1,0:T(8,128)(2,1)S(1)} async-done(((bf16[64,5,3456]{2,1,0:T(8,128)(2,1)}), bf16[64,5,3456]{2,1,0:T(8,128)(2,1)S(1)}, u32[]{:S(2)}, u32[]{:S(2)}) %all-to-all-start.3) | async-done | bytes 2211872 | tf_op jit(solution)/shard_map/all_to_all | solution.py:56
  337.2 16.6 %reshape.207 = bf16[320,64,54]{2,1,0:T(8,128)(2,1)} reshape(bf16[64,5,3456]{2,1,0:T(8,128)(2,1)S(1)} %all-to-all-done.3) | data formatting | bytes 4423680 | tf_op jit(solution)/shard_map/reshape | solution.py:42
  353.9 3.9 fusion.19
  359.2 234.1 %scatter_custom_fusion = f32[43520]{0:T(1024)S(1)} fusion(s32[34560]{0:T(1024)} %add_reduce_fusion, f32[34560]{0:T(1024)S(1)} %pad_maximum_fusion.1, f32[]{:T(128)} %constant.21.clone.1), kind=kCustom, calls=%fused_computation.19 | custom fusion | flops 34560 | bytes 174592 | tf_op jit(solution)/shard_map/add | solution.py:31
  593.8 4.9 scatter_custom_fusion.1
  598.7 101.3 %all-reduce.2 = bf16[136,5376]{0,1:T(8,128)(2,1)S(1)} all-reduce(f32[136,5376]{0,1:T(8,128)} %scatter_custom_fusion.1), channel_id=2, replica_groups=mesh['band'=64,'lev'=4] {'lev'}, use_global_device_ids=true, to_apply=%region_2.3.clone | all-reduce | flops 731136 | bytes 4386816
  703.5 9.3 %convolution_convert_fusion = bf16[68,2560]{1,0:T(8,128)(2,1)S(1)} fusion(bf16[68,2688]{1,0:T(8,128)(2,1)S(1)} %reshape.211, bf16[2688,2560]{0,1:T(8,128)(2,1)} %convert_element_type.42), kind=kOutput, calls=%fused_computation.12 | convolution fusion | flops 936028160 | bytes 14476288 | tf_op jit(solution)/shard_map/dot_general | solution.py:71
  716.0 20.0 %all_to_all.81 = bf16[64,2,1360]{2,1,0:T(2,128)(2,1)S(1)} all-to-all(bf16[64,2,1360]{2,1,0:T(2,128)(2,1)S(1)} %reshape.656), channel_id=1, replica_groups=mesh['band'=64,'lev'=4] {'band'}, dimensions={0} | all-to-all | bytes 696320 | tf_op jit(solution)/shard_map/all_to_all | solution.py:75
  (128 shorter events, 75.3 us)
Async XLA Ops:
  1.4 168.8 %all-to-all-start.2 = ((s32[64,1,1]{2,1,0:T(1,128)}), s32[64,1,1]{2,1,0:T(1,128)S(1)}, u32[]{:S(2)}, u32[]{:S(2)}) async-start(s32[64,1,1]{2,1,0:T(1,128)} %copy.36), calls=%async_computation.2 | async-start | bytes 65536 | tf_op jit(solution)/shard_map/all_to_all | solution.py:61
  26.4 60.1 %copy-start.9 = (s32[320]{0:T(512)S(1)}, s32[320]{0:T(512)}, u32[]{:S(2)}) copy-start(s32[320]{0:T(512)} %param.10) | copy-start | bytes 3844
  26.4 60.8 %copy-start.7 = (bf16[320,64]{0,1:T(8,128)(2,1)S(1)}, bf16[320,64]{0,1:T(8,128)(2,1)}, u32[]{:S(2)}) copy-start(bf16[320,64]{0,1:T(8,128)(2,1)} %param.7) | copy-start | bytes 122884
  26.4 61.8 %copy-start.8 = (bf16[320,54]{0,1:T(8,128)(2,1)S(1)}, bf16[320,54]{0,1:T(8,128)(2,1)}, u32[]{:S(2)}) copy-start(bf16[320,54]{0,1:T(8,128)(2,1)} %param.9) | copy-start | bytes 103684
  89.1 13.7 %copy-start.6 = (s32[320,54]{0,1:T(8,128)S(1)}, s32[320,54]{0,1:T(8,128)}, u32[]{:S(2)}) copy-start(s32[320,54]{0,1:T(8,128)} %param.8) | copy-start | bytes 207364
  89.1 14.7 %copy-start = (bf16[320,3456]{1,0:T(8,128)(2,1)S(1)}, bf16[320,3456]{1,0:T(8,128)(2,1)}, u32[]{:S(2)}) copy-start(bf16[320,3456]{1,0:T(8,128)(2,1)} %param.6) | copy-start | bytes 6635524
  142.2 38.2 %copy-start.10 = (u32[256]{0:T(256)S(1)}, u32[256]{0:T(256)}, u32[]{:S(2)}) copy-start(u32[256]{0:T(256)} %constant.120) | copy-start | bytes 3076
  170.1 79.9 %copy-start.5 = (s32[64,1,1]{2,1,0:T(1,128)}, s32[64,1,1]{2,1,0:T(1,128)S(1)}, u32[]{:S(2)}) copy-start(s32[64,1,1]{2,1,0:T(1,128)S(1)} %all-to-all-done.2) | copy-start | bytes 772
  170.1 19.6 %all-to-all-start = ((s32[64,5,1]{1,2,0:T(1,128)}), s32[64,5,1]{1,2,0:T(1,128)S(1)}, u32[]{:S(2)}, u32[]{:S(2)}) async-start(s32[64,5,1]{1,2,0:T(1,128)} %bitcast), calls=%async_computation | async-start | bytes 65536 | tf_op jit(solution)/shard_map/all_to_all | solution.py:60
  189.8 0.6 copy-start.4
  190.4 24.0 %all-to-all-start.5 = ((bf16[64,2,135]{2,1,0:T(2,128)(2,1)}), bf16[64,2,135]{2,1,0:T(2,128)(2,1)S(1)}, u32[]{:S(2)}, u32[]{:S(2)}) async-start(bf16[64,2,135]{2,1,0:T(2,128)(2,1)} %reshape.650), calls=%async_computation.5 | async-start | bytes 131072 | tf_op jit(solution)/shard_map/all_to_all | solution.py:59
  214.4 20.2 %copy-start.2 = (bf16[64,2,135]{2,1,0:T(2,128)(2,1)}, bf16[64,2,135]{2,1,0:T(2,128)(2,1)S(1)}, u32[]{:S(2)}) copy-start(bf16[64,2,135]{2,1,0:T(2,128)(2,1)S(1)} %all-to-all-done.5) | copy-start | bytes 103684
  214.4 20.2 %all-to-all-start.4 = ((bf16[64,2,160]{2,1,0:T(2,128)(2,1)}), bf16[64,2,160]{2,1,0:T(2,128)(2,1)S(1)}, u32[]{:S(2)}, u32[]{:S(2)}) async-start(bf16[64,2,160]{2,1,0:T(2,128)(2,1)} %reshape.654), calls=%async_computation.4 | async-start | bytes 131072 | tf_op jit(solution)/shard_map/all_to_all | solution.py:57
  234.7 0.6 copy-start.3
  235.3 14.7 %all-to-all-start.1 = ((s32[64,1,270]{2,1,0:T(1,128)}), s32[64,1,270]{2,1,0:T(1,128)S(1)}, u32[]{:S(2)}, u32[]{:S(2)}) async-start(s32[64,1,270]{2,1,0:T(1,128)} %reshape.652), calls=%async_computation.1 | async-start | bytes 196608 | tf_op jit(solution)/shard_map/all_to_all | solution.py:58
  250.0 0.6 copy-start.1
  250.7 86.6 %all-to-all-start.3 = ((bf16[64,5,3456]{2,1,0:T(8,128)(2,1)}), bf16[64,5,3456]{2,1,0:T(8,128)(2,1)S(1)}, u32[]{:S(2)}, u32[]{:S(2)}) async-start(bf16[64,5,3456]{2,1,0:T(8,128)(2,1)} %all_to_all.63), calls=%async_computation.3 | async-start | bytes 7077888 | tf_op jit(solution)/shard_map/all_to_all | solution.py:56
where the time goes:
time: 745 us; the launch traced here: 742 us
  other arithmetic  393 us (53%)
  blocking collectives  121 us (16%)
  local copies, waits for them, and re-layouts  119 us (16%)
  starting transfers between devices  47.5 us (6%)
  waiting for transfers between devices  47.1 us (6%)
  matrix products  13.3 us (2%)
    add x1, other arithmetic, profiles(): summed + jax.ops.segment_sum(upper_terms, lower_ids + 1, num_segments=rec...  234 us
    unnamed x1, blocking collectives  101 us
    another operation x2, other arithmetic  60.1 us
    lt x1, other arithmetic, contract_rows(): usable = record_ids % capacity < counts_rows[record_ids // capacity]  37.5 us
    gather x58, other arithmetic, contract_rows(): usable = record_ids % capacity < counts_rows[record_ids // capacity]  36.3 us
    another operation x1, local copies, waits for them, and re-layouts, dft_table(): stacked = jnp.stack([jnp.cos(angles), -jnp.sin(angles)], axis=2)  35.8 us
    convert_element_type x1, local copies, waits for them, and re-layouts, dft_table(): return stacked.reshape(NLON, 2 * NM).astype(jnp.bfloat16)  27.9 us
    all_to_all x1, waiting for transfers between devices, local(): lax.all_to_all(jacobian, 'band', split_axis=0, concat_axis=0, tiled=True)  21.6 us
  transfers between devices with their start and end apart: 6, of which 4 were waited for; matrix products, arithmetic and copies ran while one was open for 31% of the time, Pallas kernels for 0%

commit v1 on v0

v1 whole, which is shorter than its diff:
```python
import functools
import math

import jax
import jax.numpy as jnp
from jax import lax
from jax.experimental import pallas as pl
from jax.experimental.pallas import tpu as pltpu
from jax.sharding import PartitionSpec as P

KL = 54
KP = 56
LEVELS = 136
SHARE = 34
NLON = 2688
ROWS = 2
CAP = 5
CHANNELS = 64
WIDTH = CHANNELS * KL
RECS = 320
GROUP = 40
GROUPS = 8
ZS = 8
READERS = 64
CHUNKS = 22
LANES = 128
COEFS = 384
BLOCKS = 12
LOW = 32

F32 = jnp.float32
BF16 = jnp.bfloat16

SIN_TERMS = (
    math.pi,
    -(math.pi**3) / 6.0,
    math.pi**5 / 120.0,
    -(math.pi**7) / 5040.0,
    math.pi**9 / 362880.0,
)
MAGIC = 12582912.0


def dot_nt(a, b):
    return lax.dot_general(a, b, (((1,), (1,)), ((), ())), preferred_element_type=F32)


def dot_tn(a, b):
    return lax.dot_general(a, b, (((0,), (0,)), ((), ())), preferred_element_type=F32)


def lane_iota(shape):
    return lax.broadcasted_iota(jnp.int32, shape, 1)


def row_iota(shape):
    return lax.broadcasted_iota(jnp.int32, shape, 0)


def floor_div(values, divisor):
    return jnp.floor((values.astype(F32) + 0.5) * (1.0 / divisor))


def contract_kernel(jac_ref, dep_ref, out_ref):
    position = lane_iota((8, WIDTH))
    channel = floor_div(position, KL)
    level = position.astype(F32) - KL * channel
    spread = jnp.concatenate(
        [
            jnp.where(channel == (row_iota((8, WIDTH)) + 8 * t).astype(F32), 1.0, 0.0)
            for t in range(CHANNELS // 8)
        ],
        axis=0,
    ).astype(BF16)
    select = jnp.concatenate(
        [
            jnp.where(level == (row_iota((8, WIDTH)) + 8 * t).astype(F32), 1.0, 0.0)
            for t in range(KP // 8)
        ],
        axis=0,
    ).astype(BF16)
    for start, size in ((0, 128), (128, 128), (256, 64)):
        rows = slice(start, start + size)
        wide = jnp.dot(dep_ref[rows, :], spread, preferred_element_type=F32)
        product = jac_ref[rows, :].astype(F32) * wide
        high = product.astype(BF16)
        low = (product - high.astype(F32)).astype(BF16)
        out_ref[:, rows] = dot_nt(select, high) + dot_nt(select, low)


def prepare_kernel(index_ref, weight_ref, column_ref, count_ref, place_ref, aux_ref):
    eye = jnp.where(row_iota((KP, KL)) == lane_iota((KP, KL)), 1.0, 0.0).astype(BF16)
    place_ref[...] = dot_nt(eye, index_ref[...].astype(F32).astype(BF16)) + dot_nt(
        eye, weight_ref[...]
    )
    lanes = lane_iota((8, RECS))
    band = floor_div(lanes, CAP)
    slot = lanes.astype(F32) - CAP * band
    repeat = jnp.where(
        floor_div(lane_iota((READERS, RECS)), CAP) == row_iota((READERS, RECS)).astype(F32),
        1.0,
        0.0,
    ).astype(BF16)
    counts = jnp.broadcast_to(count_ref[...].astype(F32), (8, READERS)).astype(BF16)
    counts = jnp.dot(counts, repeat, preferred_element_type=F32)
    live = jnp.where(slot < counts, 1.0, 0.0)
    column = jnp.broadcast_to(column_ref[...], (8, RECS)) - band.astype(jnp.int32) * (ROWS * NLON)
    high = lax.shift_right_logical(column, 5)
    low = column - high * LOW
    which = row_iota((8, RECS))
    aux_ref[...] = jnp.where(
        which == 0, live, jnp.where(which == 2, high.astype(F32), low.astype(F32))
    )


def pack_kernel(own_ref, one_ref, two_ref, three_ref, place_ref, aux_ref, out_ref, sum_ref):
    sum_ref[...] = (own_ref[...] + one_ref[...]) + (two_ref[...] + three_ref[...])
    first = lax.axis_index("lev") * SHARE
    live = aux_ref[0:1, :]
    blocks = []
    for start, size in ((0, 16), (16, 16), (32, 8)):
        target = (row_iota((size, RECS)) + (first + start)).astype(F32)
        total = jnp.zeros((size, RECS), F32)
        for k in range(KL):
            hat = jnp.maximum(1.0 - jnp.abs(target - place_ref[k : k + 1, :]), 0.0)
            total = total + hat * sum_ref[k : k + 1, :]
        blocks.append(total * live)
    which = row_iota((8, RECS))
    last = jnp.where(which < 2, blocks[2], jnp.where(which < 4, aux_ref[...], 0.0))
    blocks[2] = jnp.concatenate([last, jnp.zeros((8, RECS), F32)], axis=0)
    padding = jnp.zeros((16, COEFS - RECS), F32)
    blocks = [jnp.concatenate([block, padding], axis=1) for block in blocks]
    lanes = lane_iota((16, LANES))
    for g in range(GROUPS):
        parts = [
            pltpu.roll(block, (GROUP * (t - g)) % COEFS, 1)[:, :LANES]
            for t, block in enumerate(blocks)
        ]
        message = jnp.where(
            lanes < GROUP,
            parts[0],
            jnp.where(
                lanes < 2 * GROUP, parts[1], jnp.where(lanes < 3 * GROUP, parts[2], 0.0)
            ),
        ).astype(BF16)
        for z in range(ZS):
            out_ref[(g // 2) * 16 + z * 2 + g % 2] = message


def transform_kernel(in_ref, out_ref, block_ref, acc_ref):
    z = lax.rem(lax.axis_index("band") // 2, ZS)
    lanes = lane_iota((16, LANES))
    lane = lane_iota((8, COEFS))
    tile = lane // LANES
    inside = lane - tile * LANES
    slot = floor_div(inside, GROUP).astype(jnp.int32)
    within = inside - slot * GROUP
    owner = tile * 3 + slot
    wave = (owner // 2) * 320 + (owner % 2) * 20 + z * 40 + within // 2
    wave = jnp.minimum(wave, 1279)
    odd = (within % 2).astype(F32)
    residue = wave.astype(F32) - 84.0 * floor_div(wave, 84)
    upper = (wave // 64) * 64
    which = row_iota((8, COEFS))
    factors = jnp.where(
        which == 0,
        residue * LOW,
        jnp.where(
            which == 1,
            upper.astype(F32),
            jnp.where(
                which == 2,
                (wave - upper).astype(F32),
                jnp.where(which == 3, odd * (NLON // 4), 0.0),
            ),
        ),
    ).astype(BF16)
    acc_ref[...] = jnp.zeros_like(acc_ref)
    band2 = floor_div(lanes - floor_div(lanes, GROUP).astype(jnp.int32) * GROUP, CAP) * 2.0
    step_rows = row_iota((16, LANES)).astype(F32)

    for v in range(CHUNKS):
        messages = [
            in_ref[3 * v + s].astype(F32) if 3 * v + s < READERS else jnp.zeros((16, LANES), F32)
            for s in range(3)
        ]
        for t in range(3):
            parts = [pltpu.roll(messages[s], (GROUP * (s - t)) % LANES, 1) for s in range(3)]
            block_ref[t] = jnp.where(
                lanes < GROUP,
                parts[0],
                jnp.where(
                    lanes < 2 * GROUP, parts[1], jnp.where(lanes < 3 * GROUP, parts[2], 0.0)
                ),
            )
        high = block_ref[2, 2:3, :]
        low = block_ref[2, 3:4, :]
        which = row_iota((8, LANES))
        numbers = jnp.where(
            which == 0,
            jnp.broadcast_to(high, (8, LANES)),
            jnp.where(
                which < 3,
                jnp.broadcast_to(low, (8, LANES)),
                jnp.where(which == 3, 1.0, 0.0),
            ),
        ).astype(BF16)
        turns = dot_tn(numbers, factors) * (1.0 / NLON)
        turns = turns - ((turns + MAGIC) - MAGIC)
        square = turns * turns
        series = SIN_TERMS[4]
        for term in SIN_TERMS[3::-1]:
            series = series * square + term
        sine = series * turns
        table = (1.0 - 2.0 * (sine * sine)).astype(BF16)
        row = band2 + jnp.where(jnp.broadcast_to(high, (16, LANES)) >= 84.0, 1.0, 0.0)
        mask = jnp.where(row == step_rows, 1.0, 0.0)
        left = jnp.concatenate(
            [
                (mask * jnp.broadcast_to(block_ref[n // 16, n % 16 : n % 16 + 1, :], (16, LANES)))
                for n in range(SHARE)
            ],
            axis=0,
        ).astype(BF16)
        acc_ref[...] += jnp.dot(left, table, preferred_element_type=F32)

    for d in range(GROUPS):
        tile, slot = d // 3, d % 3
        for i in range(BLOCKS):
            parts = [
                pltpu.roll(
                    acc_ref[
                        pl.ds((t * BLOCKS + i) * 16, 16), LANES * tile : LANES * (tile + 1)
                    ],
                    (GROUP * (t - slot)) % LANES,
                    1,
                )
                if t * BLOCKS + i < SHARE
                else jnp.zeros((16, LANES), F32)
                for t in range(3)
            ]
            out_ref[d, i] = jnp.where(
                lanes < GROUP, parts[0], jnp.where(lanes < 2 * GROUP, parts[1], parts[2])
            ).astype(BF16)


def place_kernel(in_ref, out_ref):
    for i in range(BLOCKS):
        for g in range(GROUPS):
            values = in_ref[g, i].astype(F32)
            for t in range(3):
                if t * BLOCKS + i < SHARE:
                    moved = pltpu.roll(values, (-GROUP * t) % LANES, 1) if t else values
                    out_ref[t * BLOCKS + i, 16 * g : 16 * g + 16, :] = moved[:, :GROUP].astype(BF16)


def call(kernel, out_shape, scratch=(), **keywords):
    return pl.pallas_call(
        kernel,
        out_shape=out_shape,
        scratch_shapes=list(scratch),
        compiler_params=pltpu.CompilerParams(vmem_limit_bytes=32 * 1024 * 1024),
        **keywords,
    )


def local(jacobian, departures, level_index, level_weight, column_index, record_counts):
    partial = call(contract_kernel, jax.ShapeDtypeStruct((KP, RECS), F32))(jacobian, departures)
    others = [
        lax.ppermute(partial, "lev", [(i, (i + k) % 4) for i in range(4)]) for k in (2, 1, 3)
    ]
    place, aux = call(
        prepare_kernel,
        (jax.ShapeDtypeStruct((KP, RECS), F32), jax.ShapeDtypeStruct((8, RECS), F32)),
    )(level_index, level_weight, column_index.reshape(1, RECS), record_counts.reshape(1, READERS))
    packed = call(
        pack_kernel,
        jax.ShapeDtypeStruct((READERS, 16, LANES), BF16),
        [pltpu.VMEM((KP, RECS), F32)],
    )(partial, *others, place, aux)
    arrived = lax.all_to_all(packed, "band", split_axis=0, concat_axis=0, tiled=True)
    spectra = call(
        transform_kernel,
        jax.ShapeDtypeStruct((GROUPS, BLOCKS, 16, LANES), BF16),
        [pltpu.VMEM((3, 16, LANES), F32), pltpu.VMEM((SHARE * 16, COEFS), F32)],
    )(arrived)
    groups = [[x * 16 + z * 2 + c for x in range(4) for c in range(2)] for z in range(ZS)]
    spectra = lax.all_to_all(
        spectra, "band", split_axis=0, concat_axis=0, axis_index_groups=groups, tiled=True
    )
    return call(place_kernel, jax.ShapeDtypeStruct((SHARE, 128, GROUP), BF16))(spectra)


def solution(mesh):
    placed = (
        P("band", "lev"),
        P("band", "lev"),
        P("band", None),
        P("band", None),
        P("band"),
        P("band"),
    )
    return jax.shard_map(
        local, mesh=mesh, in_specs=placed, out_specs=P("lev", None, "band"), check_vma=False
    )
```

time: 745 us -> 62.5 us (0.08)
  other arithmetic: 393 us -> 0 us
  local copies, waits for them, and re-layouts: 119 us -> 3.93 us
  blocking collectives: 121 us -> 37.9 us
  waiting for transfers between devices: 47.1 us -> 3.55 us
  starting transfers between devices: 47.5 us -> 5.28 us
  matrix products: 13.3 us -> 0 us
  Pallas kernels: 0 us -> 11.5 us
    add x2 -> x0, other arithmetic: 235 us -> none  [the longest x1 234 us: profiles(): summed + jax.ops.segment_sum(upper_terms, lower_ids + 1, num_segments=rec...]
    unnamed x1 -> x0, blocking collectives: 101 us -> none
    another operation x3 -> x0, other arithmetic: 72.8 us -> none
    all_to_all x6 -> x0, starting transfers between devices: 47.5 us -> none  [the longest x1 13 us: local(): lax.all_to_all(record_counts, 'band', split_axis=0, concat_axis=0, tiled=...]
    all_to_all x6 -> x0, waiting for transfers between devices: 47.1 us -> none  [the longest x1 21.6 us: local(): lax.all_to_all(jacobian, 'band', split_axis=0, concat_axis=0, tiled=True)]
    lt x1 -> x0, other arithmetic: 37.5 us -> none  [contract_rows(): usable = record_ids % capacity < counts_rows[record_ids // capacity]]
    gather x58 -> x0, other arithmetic: 36.3 us -> none  [contract_rows(): usable = record_ids % capacity < counts_rows[record_ids // capacity]]
    another operation x1 -> x0, local copies, waits for them, and re-layouts: 35.8 us -> none  [dft_table(): stacked = jnp.stack([jnp.cos(angles), -jnp.sin(angles)], axis=2)]
  transfers between devices with their start and end apart: 6 -> 3, of which waited for: 4 -> 1; matrix products, arithmetic and copies ran while one was open for 31% -> 0% of each run, Pallas kernels for 0% -> 0%
where the time goes in v1:
time: 62.5 us; the launch traced here: 62.3 us
  blocking collectives  37.9 us (61%)
  Pallas kernels  11.5 us (18%)
  starting transfers between devices  5.28 us (8%)
  local copies, waits for them, and re-layouts  3.93 us (6%)
  waiting for transfers between devices  3.55 us (6%)
    all_to_all x1, blocking collectives, local(): lax.all_to_all(packed, 'band', split_axis=0, concat_axis=0, tiled=True)  25.6 us
    all_to_all x1, blocking collectives, local(): lax.all_to_all(spectra, 'band', split_axis=0, concat_axis=0, axis_index_g...  12.3 us
    pallas_call x1, Pallas kernels, local(): call(transform_kernel, jax.ShapeDtypeStruct((GROUPS, BLOCKS, 16, LANES),...  7.88 us
    ppermute x3, starting transfers between devices, local(): lax.ppermute(partial, 'lev', [(i, (i + k) % 4) for i in range(4)])  5.28 us
    ppermute x3, waiting for transfers between devices, local(): lax.ppermute(partial, 'lev', [(i, (i + k) % 4) for i in range(4)])  3.55 us
    unnamed x13, local copies, waits for them, and re-layouts  2.83 us
    pallas_call x1, Pallas kernels, local(): call(contract_kernel, jax.ShapeDtypeStruct((KP, RECS), F32))  2.42 us
  transfers between devices with their start and end apart: 3, of which 1 were waited for; matrix products, arithmetic and copies ran while one was open for 0% of the time, Pallas kernels for 0%

profile of v1, /device:TPU:1, one launch (start us, length us, event | category | flops | bytes accessed | tf_op | source)
XLA Modules:
  0.0 62.3 jit_solution(1747491979575532985)
XLA Ops:
  0.0 0.0 copy-start.3
  0.0 0.9 %copy.7.dep_ref = bf16[320,64]{1,0:T(8,128)(2,1)S(1)} copy(bf16[320,64]{0,1:T(8,128)(2,1)} %param.7) | data formatting | bytes 81920 | tf_op args[1]
  1.0 0.0 copy-start
  1.0 1.6 %copy-done = bf16[320,3456]{1,0:T(8,128)(2,1)S(1)} copy-done((bf16[320,3456]{1,0:T(8,128)(2,1)S(1)}, bf16[320,3456]{1,0:T(8,128)(2,1)}, u32[]{:S(2)}) %copy-start) | copy-done | bytes 2211864
  2.6 2.4 %shard_map.64.own_ref = f32[56,320]{1,0:T(8,128)S(1)} custom-call(bf16[320,3456]{1,0:T(8,128)(2,1)S(1)} %copy-done, bf16[320,64]{1,0:T(8,128)(2,1)S(1)} %copy.7.dep_ref), custom_call_target="tpu_custom_call" | custom-call | tf_op jit(solution)/shard_map/pallas_call | solution.py:268
  5.0 3.6 %collective-permute-start.2 = (f32[56,320]{1,0:T(8,128)S(1)}, f32[56,320]{1,0:T(8,128)S(1)}, u32[]{:S(2)}, u32[]{:S(2)}) collective-permute-start(f32[56,320]{1,0:T(8,128)S(1)} %shard_map.64.own_ref), channel_id=1, source_target_pairs={{0,3},{1,0},{2,1},{3,2},{4,7},{5,4},{6,5},{7,6},{8,11},{9,8},{10,9... | collective-permute-start | bytes 215048 | tf_op jit(solution)/shard_map/ppermute | solution.py:270
  8.6 0.0 collective-permute-start.1
  8.7 1.6 %collective-permute-start = (f32[56,320]{1,0:T(8,128)S(1)}, f32[56,320]{1,0:T(8,128)S(1)}, u32[]{:S(2)}, u32[]{:S(2)}) collective-permute-start(f32[56,320]{1,0:T(8,128)S(1)} %shard_map.64.own_ref), channel_id=1, source_target_pairs={{0,2},{1,3},{2,0},{3,1},{4,6},{5,7},{6,4},{7,5},{8,10},{9,11},{10,... | collective-permute-start | bytes 215048 | tf_op jit(solution)/shard_map/ppermute | solution.py:270
  10.3 0.0 copy-done.4
  10.3 0.0 copy-done.3
  10.3 0.1 copy.9.weight_ref
  10.4 0.0 copy-done.2
  10.4 0.1 copy.8.index_ref
  10.6 0.0 copy-done.1
  10.6 0.2 shard_map.65
  10.8 0.0 collective-permute-done.2.three_ref
  10.8 3.5 %collective-permute-done.1.two_ref = f32[56,320]{1,0:T(8,128)S(1)} collective-permute-done((f32[56,320]{1,0:T(8,128)S(1)}, f32[56,320]{1,0:T(8,128)S(1)}, u32[]{:S(2)}, u32[]{:S(2)}) %collective-permute-start.1) | collective-permute-done | bytes 71712 | tf_op jit(solution)/shard_map/ppermute | solution.py:270
  14.3 0.0 collective-permute-done.one_ref
  14.3 0.8 %shard_map.66 = bf16[64,16,128]{2,1,0:T(8,128)(2,1)S(1)} custom-call(f32[56,320]{1,0:T(8,128)S(1)} %shard_map.64.own_ref, f32[56,320]{1,0:T(8,128)S(1)} %collective-permute-done.one_ref, f32[56,320]{1,0:T(8,128)S(1)} %collective-permute-done.1.two_ref, f32[56,320]{1,0:T(8,128)S(1)} %collective-permute-done.2.three_ref, ...), custom_call_target="tpu_custom_call" | custom-call | tf_op jit(solution)/shard_map/pallas_call | solution.py:276
  15.1 25.6 %all_to_all.10.in_ref = bf16[64,16,128]{2,1,0:T(8,128)(2,1)S(1)} all-to-all(bf16[64,16,128]{2,1,0:T(8,128)(2,1)S(1)} %shard_map.66), channel_id=1, replica_groups=mesh['band'=64,'lev'=4] {'band'}, dimensions={0} | all-to-all | bytes 524288 | tf_op jit(solution)/shard_map/all_to_all | solution.py:281
  40.7 7.9 %shard_map.67 = bf16[8,12,16,128]{3,2,1,0:T(8,128)(2,1)S(1)} custom-call(bf16[64,16,128]{2,1,0:T(8,128)(2,1)S(1)} %all_to_all.10.in_ref), custom_call_target="tpu_custom_call" | custom-call | tf_op jit(solution)/shard_map/pallas_call | solution.py:282
  48.6 12.3 %all_to_all.11.in_ref = bf16[8,12,16,128]{3,2,1,0:T(8,128)(2,1)S(1)} all-to-all(bf16[8,12,16,128]{3,2,1,0:T(8,128)(2,1)S(1)} %shard_map.67), channel_id=1, replica_groups={{0,4,64,68,128,132,192,196},{8,12,72,76,136,140,200,204},{16,20,80,84,1..., dimensions={0} | all-to-all | bytes 786432 | tf_op jit(solution)/shard_map/all_to_all | solution.py:288
  60.9 0.3 shard_map.68
  61.2 1.1 %copy.10 = bf16[34,128,40]{1,2,0:T(8,128)(2,1)} copy(bf16[34,128,40]{2,1,0:T(8,128)(2,1)S(1)} %shard_map.68) | data formatting | bytes 696320 | tf_op jit(solution)/shard_map/pallas_call | solution.py:291
  (4 shorter events, 0.0 us)
Async XLA Ops:
  0.0 10.3 %copy-start.3 = (bf16[320,54]{0,1:T(8,128)(2,1)S(1)}, bf16[320,54]{0,1:T(8,128)(2,1)}, u32[]{:S(2)}) copy-start(bf16[320,54]{0,1:T(8,128)(2,1)} %param.9) | copy-start | bytes 103684
  0.0 10.4 %copy-start.2 = (s32[320,54]{0,1:T(8,128)S(1)}, s32[320,54]{0,1:T(8,128)}, u32[]{:S(2)}) copy-start(s32[320,54]{0,1:T(8,128)} %param.8) | copy-start | bytes 207364
  0.0 10.6 %copy-start.1 = (s32[64]{0:T(128)S(1)}, s32[64]{0:T(128)}, u32[]{:S(2)}) copy-start(s32[64]{0:T(128)} %param.11) | copy-start | bytes 772
  1.0 1.6 %copy-start = (bf16[320,3456]{1,0:T(8,128)(2,1)S(1)}, bf16[320,3456]{1,0:T(8,128)(2,1)}, u32[]{:S(2)}) copy-start(bf16[320,3456]{1,0:T(8,128)(2,1)} %jac_ref.1) | copy-start | bytes 6635524
  2.6 7.7 %copy-start.4 = (s32[320]{0:T(512)S(1)}, s32[320]{0:T(512)}, u32[]{:S(2)}) copy-start(s32[320]{0:T(512)} %param.10) | copy-start | bytes 3844
  5.0 5.8 %collective-permute-start.2 = (f32[56,320]{1,0:T(8,128)S(1)}, f32[56,320]{1,0:T(8,128)S(1)}, u32[]{:S(2)}, u32[]{:S(2)}) collective-permute-start(f32[56,320]{1,0:T(8,128)S(1)} %shard_map.64.own_ref), channel_id=1, source_target_pairs={{0,3},{1,0},{2,1},{3,2},{4,7},{5,4},{6,5},{7,6},{8,11},{9,8},{10,9... | collective-permute-start | bytes 215048 | tf_op jit(solution)/shard_map/ppermute | solution.py:270
  8.6 5.6 %collective-permute-start.1 = (f32[56,320]{1,0:T(8,128)S(1)}, f32[56,320]{1,0:T(8,128)S(1)}, u32[]{:S(2)}, u32[]{:S(2)}) collective-permute-start(f32[56,320]{1,0:T(8,128)S(1)} %shard_map.64.own_ref), channel_id=1, source_target_pairs={{0,1},{1,2},{2,3},{3,0},{4,5},{5,6},{6,7},{7,4},{8,9},{9,10},{10,1... | collective-permute-start | bytes 215048 | tf_op jit(solution)/shard_map/ppermute | solution.py:270
  8.7 5.7 %collective-permute-start = (f32[56,320]{1,0:T(8,128)S(1)}, f32[56,320]{1,0:T(8,128)S(1)}, u32[]{:S(2)}, u32[]{:S(2)}) collective-permute-start(f32[56,320]{1,0:T(8,128)S(1)} %shard_map.64.own_ref), channel_id=1, source_target_pairs={{0,2},{1,3},{2,0},{3,1},{4,6},{5,7},{6,4},{7,5},{8,10},{9,11},{10,... | collective-permute-start | bytes 215048 | tf_op jit(solution)/shard_map/ppermute | solution.py:270

commit v2 on v1

v2 whole, which is shorter than its diff:
```python
import math

import jax
import jax.numpy as jnp
from jax import lax
from jax.experimental import pallas as pl
from jax.experimental.pallas import tpu as pltpu
from jax.sharding import PartitionSpec as P

KL = 54
KP = 56
SHARE = 34
NLON = 2688
ROWS = 2
CAP = 5
CHANNELS = 64
WIDTH = CHANNELS * KL
RECS = 320
PIECES = ((0, 128), (128, 128), (256, 64))
GROUP = 40
GROUPS = 8
XS = 4
ZS = 8
CORES = 2
BANDS = 64
SENDERS = XS * ZS
TILES = 11
LANES = 128
DEPTH = CORES * TILES * LANES
COEFS = 40
PARTS = 5
TOGETHER = 8
LOW = 32

F32 = jnp.float32
BF16 = jnp.bfloat16

SIN_TERMS = (
    math.pi,
    -(math.pi**3) / 6.0,
    math.pi**5 / 120.0,
    -(math.pi**7) / 5040.0,
    math.pi**9 / 362880.0,
)
MAGIC = 12582912.0


def dot_nt(a, b):
    return lax.dot_general(a, b, (((1,), (1,)), ((), ())), preferred_element_type=F32)


def dot_tn(a, b):
    return lax.dot_general(a, b, (((0,), (0,)), ((), ())), preferred_element_type=F32)


def lane_iota(shape):
    return lax.broadcasted_iota(jnp.int32, shape, 1)


def row_iota(shape):
    return lax.broadcasted_iota(jnp.int32, shape, 0)


def floor_div(values, divisor):
    return jnp.floor((values.astype(F32) + 0.5) * (1.0 / divisor))


def contract_kernel(jac_hbm, dep_ref, out_ref, jac_ref, wide_ref, semaphores):
    copies = [
        pltpu.make_async_copy(
            jac_hbm.at[pl.ds(start, size)], jac_ref.at[pl.ds(start, size)], semaphores.at[p]
        )
        for p, (start, size) in enumerate(PIECES)
    ]
    for copy in copies:
        copy.start()
    position = lane_iota((8, WIDTH))
    channel = floor_div(position, KL)
    level = position.astype(F32) - KL * channel
    spread = jnp.concatenate(
        [
            jnp.where(channel == (row_iota((8, WIDTH)) + 8 * t).astype(F32), 1.0, 0.0)
            for t in range(CHANNELS // 8)
        ],
        axis=0,
    ).astype(BF16)
    select = jnp.concatenate(
        [
            jnp.where(level == (row_iota((8, WIDTH)) + 8 * t).astype(F32), 1.0, 0.0)
            for t in range(KP // 8)
        ],
        axis=0,
    ).astype(BF16)
    wide_ref[...] = dot_tn(dep_ref[...], spread)
    for copy, (start, size) in zip(copies, PIECES):
        records = slice(start, start + size)
        copy.wait()
        product = jac_ref[records, :].astype(F32) * wide_ref[records, :]
        high = product.astype(BF16)
        low = (product - high.astype(F32)).astype(BF16)
        out_ref[:, records] = dot_nt(select, high) + dot_nt(select, low)


def prepare_kernel(index_ref, weight_ref, column_ref, count_ref, place_ref, aux_ref):
    place_ref[...] = index_ref[...].astype(F32) + weight_ref[...].astype(F32)
    lanes = lane_iota((8, RECS))
    band = floor_div(lanes, CAP)
    slot = lanes.astype(F32) - CAP * band
    repeat = jnp.where(
        floor_div(lane_iota((BANDS, RECS)), CAP) == row_iota((BANDS, RECS)).astype(F32),
        1.0,
        0.0,
    ).astype(BF16)
    counts = jnp.broadcast_to(count_ref[...].astype(F32), (8, BANDS)).astype(BF16)
    counts = jnp.dot(counts, repeat, preferred_element_type=F32)
    live = jnp.where(slot < counts, 1.0, 0.0)
    column = jnp.broadcast_to(column_ref[...], (8, RECS)) - band.astype(jnp.int32) * (ROWS * NLON)
    high = lax.shift_right_logical(column, 5)
    low = column - high * LOW
    which = row_iota((8, RECS))
    aux_ref[...] = jnp.where(
        which == 0, live, jnp.where(which == 2, high.astype(F32), low.astype(F32))
    )


def pack_kernel(own_ref, one_ref, two_ref, three_ref, place_ref, aux_ref, out_ref, sum_ref):
    sum_ref[...] = (own_ref[...] + one_ref[...]) + (two_ref[...] + three_ref[...])
    first = lax.axis_index("lev") * SHARE
    live = aux_ref[0:1, :]
    blocks = []
    for start, size in ((0, 24), (24, 8), (32, 8)):
        target = (row_iota((size, RECS)) + (first + start)).astype(F32)
        total = jnp.zeros((size, RECS), F32)
        for k in range(KL):
            hat = jnp.maximum(1.0 - jnp.abs(target - place_ref[k : k + 1, :]), 0.0)
            total = total + hat * sum_ref[k : k + 1, :]
        blocks.append(total * live)
    which = row_iota((8, RECS))
    blocks[2] = jnp.where(which < 2, blocks[2], jnp.where(which < 4, aux_ref[...], 0.0))
    full = 3 * LANES
    upper, middle, last = [
        jnp.concatenate([block, jnp.zeros((block.shape[0], full - RECS), F32)], axis=1)
        for block in blocks
    ]

    def moved(block, source, target):
        return pltpu.roll(block, (target - source) % full, 1)[:, :LANES]

    lanes = lane_iota((24, LANES))
    low_rows = row_iota((8, LANES)) < 4
    for x in range(XS):
        one, two, spot = 2 * GROUP * x, 2 * GROUP * x + GROUP, 2 * GROUP
        rest = jnp.concatenate(
            [
                moved(middle, one, spot),
                moved(middle, two, spot),
                jnp.where(low_rows, moved(last, one, spot), pltpu.roll(moved(last, two, spot), 4, 0)),
            ],
            axis=0,
        )
        message = jnp.where(
            lanes < spot, moved(upper, one, 0), jnp.where(lanes < 3 * GROUP, rest, 0.0)
        ).astype(BF16)
        for z in range(ZS):
            out_ref[x * ZS + z] = message


def wave_factors(x, z, core):
    shape = (88, LANES)
    row = row_iota(shape)
    lane = lane_iota(shape)
    target = jnp.bitwise_and(row + x, 3)
    first = target * 320 + (core * 20 + z * 40)
    inner = jnp.maximum(jnp.where(row < 48, row - 8, row - 48), 0)
    step = lax.shift_right_logical(inner, 1)
    odd = inner - 2 * step
    wave = jnp.where(row < 8, first, step)
    quarter = jnp.where(
        row < 4, 0, jnp.where(row < 8, -1, jnp.where(row < 48, odd, odd - 1))
    ).astype(F32)
    residue = wave.astype(F32) - 84.0 * floor_div(wave, 84)
    lower = jnp.bitwise_and(wave, 63)
    values = jnp.where(
        lane == 0,
        residue * LOW,
        jnp.where(
            lane == 1,
            (wave - lower).astype(F32),
            jnp.where(
                lane == 2,
                lower.astype(F32),
                jnp.where(lane == 3, quarter * (NLON // 4), 0.0),
            ),
        ),
    )
    return values[:, :16].astype(BF16)


def transform_kernel(
    own_ref, other_ref, out0_ref, out1_ref, out2_ref, out3_ref, block_ref, left_ref, table_ref
):
    outs = (out0_ref, out1_ref, out2_ref, out3_ref)
    place = lax.axis_index("band")
    factors = wave_factors(place // 16, lax.rem(place // 2, ZS), lax.rem(place, 2))
    lanes8 = lane_iota((8, LANES))
    lanes = lane_iota((16, LANES))
    slot = floor_div(lanes, GROUP)
    band2 = floor_div(lanes.astype(F32) - GROUP * slot, CAP) * 2.0
    step_rows = row_iota((16, LANES)).astype(F32)
    which = row_iota((16, LANES))
    for c in range(CORES):
        left_ref[c, SHARE * 16 :, :] = jnp.zeros((PARTS * LANES - SHARE * 16, DEPTH), BF16)

    for v in range(CORES * TILES):
        half, tile = v // TILES, v % TILES
        arrived = (own_ref, other_ref)[half]
        columns = slice(LANES * v, LANES * (v + 1))
        messages = [
            arrived[3 * tile + s].astype(F32)
            if 3 * tile + s < SENDERS
            else jnp.zeros((24, LANES), F32)
            for s in range(3)
        ]
        for c in range(CORES):
            groups = []
            for s, message in enumerate(messages):
                near = (GROUP * (s - c)) % LANES
                far = (GROUP * (s - 2)) % LANES
                last = pltpu.roll(message[16:24], far, 1)
                groups.append(
                    [pltpu.roll(message[8 * t : 8 * t + 8], near, 1) for t in range(3)]
                    + [
                        pltpu.roll(message[8 * c : 8 * c + 8], far, 1),
                        pltpu.roll(last, 4, 0) if c else last,
                    ]
                )
            for t in range(5):
                block_ref[v, c, t] = jnp.where(
                    lanes8 < GROUP,
                    groups[0][t],
                    jnp.where(
                        lanes8 < 2 * GROUP,
                        groups[1][t],
                        jnp.where(lanes8 < 3 * GROUP, groups[2][t], 0.0),
                    ),
                )
            high = jnp.broadcast_to(block_ref[v, c, 4, 2:3, :], (16, LANES))
            low = jnp.broadcast_to(block_ref[v, c, 4, 3:4, :], (16, LANES))
            numbers = jnp.where(
                which == 0, high, jnp.where(which < 3, low, jnp.where(which == 3, 1.0, 0.0))
            ).astype(BF16)
            turns = jnp.dot(factors, numbers, preferred_element_type=F32) * (1.0 / NLON)
            turns = turns - ((turns + MAGIC) - MAGIC)
            square = turns * turns
            series = SIN_TERMS[4]
            for term in SIN_TERMS[3::-1]:
                series = series * square + term
            sine = series * turns
            waves = 1.0 - 2.0 * (sine * sine)
            inner_cosine, inner_sine = waves[8:48], waves[48:88]
            for pair in range(2):
                table_ref[c, 80 * pair : 80 * pair + 80, columns] = jnp.concatenate(
                    [
                        waves[d : d + 1] * inner_cosine - waves[4 + d : 5 + d] * inner_sine
                        for d in (2 * pair, 2 * pair + 1)
                    ],
                    axis=0,
                ).astype(BF16)
            row = band2 + jnp.where(high >= 84.0, 1.0, 0.0)
            mask = jnp.where(row == step_rows, 1.0, 0.0)
            for n in range(SHARE):
                left_ref[c, 16 * n : 16 * n + 16, columns] = (
                    mask * block_ref[v, c, n // 8, n % 8 : n % 8 + 1, :]
                ).astype(BF16)

    for c in range(CORES):
        for start, size in ((0, 256), (256, 256), (512, 128)):
            result = dot_nt(table_ref[c], left_ref[c, start : start + size, :])
            for part in range(size // LANES):
                for k in range(XS):
                    group = (2 * (-k % XS) + c) % GROUPS
                    piece = result[
                        COEFS * k : COEFS * (k + 1), LANES * part : LANES * (part + 1)
                    ]
                    if group:
                        piece = pltpu.roll(piece, 16 * group, 1)
                    outs[k][c, start // LANES + part] = piece.astype(BF16)


def place_kernel(zero_ref, one_ref, two_ref, three_ref, out_hbm, out_ref, semaphores):
    shift = 32 * (lax.axis_index("band") // 16)
    slot = lax.shift_right_logical(lane_iota((COEFS, LANES)), 4)
    sources = (zero_ref, three_ref, two_ref, one_ref)
    copies = []
    for part in range(PARTS):
        values = [sources[g // 2][g % 2, part].astype(F32) for g in range(GROUPS)]
        first = part * TOGETHER
        count = min(TOGETHER, SHARE - first)
        for q in range(count):
            merged = values[(-q) % TOGETHER]
            for p in range(1, TOGETHER):
                merged = jnp.where(slot == p, values[(p - q) % TOGETHER], merged)
            turn = lax.rem(shift + (LANES - 16 * q), LANES)
            out_ref[first + q] = pltpu.roll(merged, turn, 1).astype(BF16)
        copy = pltpu.make_async_copy(
            out_ref.at[pl.ds(first, count)], out_hbm.at[pl.ds(first, count)], semaphores.at[part]
        )
        copy.start()
        copies.append(copy)
    for copy in copies:
        copy.wait()


def call(kernel, out_shape, scratch=(), limit=32, **keywords):
    return pl.pallas_call(
        kernel,
        out_shape=out_shape,
        scratch_shapes=list(scratch),
        compiler_params=pltpu.CompilerParams(vmem_limit_bytes=limit * 1024 * 1024),
        **keywords,
    )


def x_shift(k):
    return [
        (x * 16 + rest, (x + k) % XS * 16 + rest) for x in range(XS) for rest in range(ZS * CORES)
    ]


def local(jacobian, departures, level_index, level_weight, column_index, record_counts):
    vmem = pl.BlockSpec(memory_space=pltpu.VMEM)
    hbm = pl.BlockSpec(memory_space=pltpu.HBM)
    partial = call(
        contract_kernel,
        jax.ShapeDtypeStruct((KP, RECS), F32),
        [
            pltpu.VMEM((RECS, WIDTH), BF16),
            pltpu.VMEM((RECS, WIDTH), F32),
            pltpu.SemaphoreType.DMA((len(PIECES),)),
        ],
        limit=59,
        in_specs=[hbm, vmem],
        out_specs=vmem,
    )(jacobian, departures.T)
    others = [
        lax.ppermute(partial, "lev", [(i, (i + k) % 4) for i in range(4)]) for k in (2, 1, 3)
    ]
    place, aux = call(
        prepare_kernel,
        (jax.ShapeDtypeStruct((KL, RECS), F32), jax.ShapeDtypeStruct((8, RECS), F32)),
    )(level_index.T, level_weight.T, column_index.reshape(1, RECS), record_counts.reshape(1, BANDS))
    packed = call(
        pack_kernel,
        jax.ShapeDtypeStruct((SENDERS, 24, LANES), BF16),
        [pltpu.VMEM((KP, RECS), F32)],
    )(partial, *others, place, aux)
    same_core = [
        [x * 16 + z * 2 + c for x in range(XS) for z in range(ZS)] for c in range(CORES)
    ]
    arrived = lax.all_to_all(
        packed, "band", split_axis=0, concat_axis=0, axis_index_groups=same_core, tiled=True
    )
    other = lax.ppermute(arrived, "band", [(i, i ^ 1) for i in range(BANDS)])
    spectra = call(
        transform_kernel,
        [jax.ShapeDtypeStruct((CORES, PARTS, COEFS, LANES), BF16)] * XS,
        [
            pltpu.VMEM((CORES * TILES, CORES, 5, 8, LANES), F32),
            pltpu.VMEM((CORES, PARTS * LANES, DEPTH), BF16),
            pltpu.VMEM((CORES, XS * COEFS, DEPTH), BF16),
        ],
    )(arrived, other)
    received = [spectra[0]] + [None] * 3
    for k in (2, 1, 3):
        received[k] = lax.ppermute(spectra[k], "band", x_shift(k))
    placed = call(
        place_kernel,
        jax.ShapeDtypeStruct((SHARE, COEFS, LANES), BF16),
        [pltpu.VMEM((SHARE, COEFS, LANES), BF16), pltpu.SemaphoreType.DMA((PARTS,))],
        in_specs=[vmem] * 4,
        out_specs=hbm,
    )(*received)
    return jnp.transpose(placed, (0, 2, 1))


def solution(mesh):
    placed = (
        P("band", "lev"),
        P("band", "lev"),
        P("band", None),
        P("band", None),
        P("band"),
        P("band"),
    )
    return jax.shard_map(
        local, mesh=mesh, in_specs=placed, out_specs=P("lev", None, "band"), check_vma=False
    )
```

time: 62.5 us -> 54.5 us (0.87)
  blocking collectives: 37.9 us -> 20.2 us
  starting transfers between devices: 5.28 us -> 12.6 us
  waiting for transfers between devices: 3.55 us -> 9.7 us
  local copies, waits for them, and re-layouts: 3.93 us -> 0.91 us
    all_to_all x2 -> x1, blocking collectives: 37.9 us -> 20.2 us  [local(): lax.all_to_all(packed, 'band', split_axis=0, concat_axis=0, axis_index_gr...]
    ppermute x0 -> x4, starting transfers between devices: none -> 7.28 us  [the longest x1 3.99 us: local(): other = lax.ppermute(arrived, 'band', [(i, i ^ 1) for i in range(BANDS)])]
    ppermute x0 -> x4, waiting for transfers between devices: none -> 5.62 us  [the longest x3 4.55 us: local(): received[k] = lax.ppermute(spectra[k], 'band', x_shift(k))]
    unnamed x13 -> x10, local copies, waits for them, and re-layouts: 2.83 us -> 0.9 us
    pallas_call x1 -> x0, local copies, waits for them, and re-layouts: 1.09 us -> none  [local(): call(place_kernel, jax.ShapeDtypeStruct((SHARE, 128, GROUP), BF16))(spectra)]
    pallas_call x5, Pallas kernels: 11.5 us -> 10.9 us  [the longest x1 4.63 us: local(): call(contract_kernel, jax.ShapeDtypeStruct((KP, RECS), F32), [pltpu.VMEM(...]
  transfers between devices with their start and end apart: 3 -> 7, of which waited for: 1 -> 5; matrix products, arithmetic and copies ran while one was open for 0% -> 0% of each run, Pallas kernels for 0% -> 0%
where the time goes in v2:
time: 54.5 us; the launch traced here: 54.3 us
  blocking collectives  20.2 us (37%)
  starting transfers between devices  12.6 us (23%)
  Pallas kernels  10.9 us (20%)
  waiting for transfers between devices  9.7 us (18%)
  local copies, waits for them, and re-layouts  0.91 us (2%)
    all_to_all x1, blocking collectives, local(): lax.all_to_all(packed, 'band', split_axis=0, concat_axis=0, axis_index_gr...  20.2 us
    ppermute x3, starting transfers between devices, local(): lax.ppermute(partial, 'lev', [(i, (i + k) % 4) for i in range(4)])  5.28 us
    pallas_call x1, Pallas kernels, local(): call(contract_kernel, jax.ShapeDtypeStruct((KP, RECS), F32), [pltpu.VMEM(...  4.63 us
    ppermute x3, waiting for transfers between devices, local(): received[k] = lax.ppermute(spectra[k], 'band', x_shift(k))  4.55 us
    pallas_call x1, Pallas kernels, local(): call(transform_kernel, [jax.ShapeDtypeStruct((CORES, PARTS, COEFS, LANES)...  4.36 us
    ppermute x3, waiting for transfers between devices, local(): lax.ppermute(partial, 'lev', [(i, (i + k) % 4) for i in range(4)])  4.08 us
    ppermute x1, starting transfers between devices, local(): other = lax.ppermute(arrived, 'band', [(i, i ^ 1) for i in range(BANDS)])  3.99 us
    ppermute x3, starting transfers between devices, local(): received[k] = lax.ppermute(spectra[k], 'band', x_shift(k))  3.29 us
  transfers between devices with their start and end apart: 7, of which 5 were waited for; matrix products, arithmetic and copies ran while one was open for 0% of the time, Pallas kernels for 0%

profile of v2, /device:TPU:1, one launch (start us, length us, event | category | flops | bytes accessed | tf_op | source)
XLA Modules:
  0.0 54.3 jit_solution(6645176129157051192)
XLA Ops:
  0.0 0.0 copy-start.1
  0.0 4.6 %shard_map.64.own_ref = f32[56,320]{1,0:T(8,128)} custom-call(bf16[320,3456]{1,0:T(8,128)(2,1)} %jac_hbm.1, bf16[64,320]{1,0:T(8,128)(2,1)} %bitcast.8), custom_call_target="tpu_custom_call" | custom-call | tf_op jit(solution)/shard_map/pallas_call | solution.py:333
  4.7 3.6 %collective-permute-start.2 = (f32[56,320]{1,0:T(8,128)}, f32[56,320]{1,0:T(8,128)S(1)}, u32[]{:S(2)}, u32[]{:S(2)}) collective-permute-start(f32[56,320]{1,0:T(8,128)} %shard_map.64.own_ref), channel_id=1, source_target_pairs={{0,3},{1,0},{2,1},{3,2},{4,7},{5,4},{6,5},{7,6},{8,11},{9,8},{10,9... | collective-permute-start | bytes 215048 | tf_op jit(solution)/shard_map/ppermute | solution.py:346
  8.3 0.0 collective-permute-start.1
  8.3 1.6 %collective-permute-start = (f32[56,320]{1,0:T(8,128)}, f32[56,320]{1,0:T(8,128)S(1)}, u32[]{:S(2)}, u32[]{:S(2)}) collective-permute-start(f32[56,320]{1,0:T(8,128)} %shard_map.64.own_ref), channel_id=1, source_target_pairs={{0,2},{1,3},{2,0},{3,1},{4,6},{5,7},{6,4},{7,5},{8,10},{9,11},{10,... | collective-permute-start | bytes 215048 | tf_op jit(solution)/shard_map/ppermute | solution.py:346
  9.9 0.0 copy-done.4
  10.0 0.0 copy-done.1
  10.0 0.1 shard_map.65
  10.1 0.0 collective-permute-done.2.three_ref
  10.1 4.0 %collective-permute-done.1.two_ref = f32[56,320]{1,0:T(8,128)S(1)} collective-permute-done((f32[56,320]{1,0:T(8,128)}, f32[56,320]{1,0:T(8,128)S(1)}, u32[]{:S(2)}, u32[]{:S(2)}) %collective-permute-start.1) | collective-permute-done | bytes 71712 | tf_op jit(solution)/shard_map/ppermute | solution.py:346
  14.1 0.0 collective-permute-done.one_ref
  14.2 0.9 %copy-done = f32[56,320]{1,0:T(8,128)S(1)} copy-done((f32[56,320]{1,0:T(8,128)S(1)}, f32[56,320]{1,0:T(8,128)}, u32[]{:S(2)}) %copy-start) | copy-done | bytes 71704
  15.1 0.8 %shard_map.66 = bf16[32,24,128]{2,1,0:T(8,128)(2,1)S(1)} custom-call(f32[56,320]{1,0:T(8,128)S(1)} %copy-done, f32[56,320]{1,0:T(8,128)S(1)} %collective-permute-done.one_ref, f32[56,320]{1,0:T(8,128)S(1)} %collective-permute-done.1.two_ref, f32[56,320]{1,0:T(8,128)S(1)} %collective-permute-done.2.three_ref, f32[54,320]{1,0:T(8,128)S(1)} %get-tuple-element.11.place_ref, ...), custom_call_target="tpu_custom_call" | custom-call | tf_op jit(solution)/shard_map/pallas_call | solution.py:352
  15.9 20.2 %all_to_all.5.own_ref = bf16[32,24,128]{2,1,0:T(8,128)(2,1)S(1)} all-to-all(bf16[32,24,128]{2,1,0:T(8,128)(2,1)S(1)} %shard_map.66), channel_id=1, replica_groups={{0,8,16,24,32,40,48,56,64,72,80,88,96,104,112,120,128,136,144,152,160,1..., dimensions={0} | all-to-all | bytes 393216 | tf_op jit(solution)/shard_map/all_to_all | solution.py:360
  36.1 4.0 %collective-permute-start.3 = (bf16[32,24,128]{2,1,0:T(8,128)(2,1)S(1)}, bf16[32,24,128]{2,1,0:T(8,128)(2,1)S(1)}, u32[]{:S(2)}, u32[]{:S(2)}) collective-permute-start(bf16[32,24,128]{2,1,0:T(8,128)(2,1)S(1)} %all_to_all.5.own_ref), channel_id=1, source_target_pairs={{0,4},{4,0},{8,12},{12,8},{16,20},{20,16},{24,28},{28,24},{32,36},... | collective-permute-start | bytes 589832 | tf_op jit(solution)/shard_map/ppermute | solution.py:363
  40.1 1.1 %collective-permute-done.3.other_ref = bf16[32,24,128]{2,1,0:T(8,128)(2,1)S(1)} collective-permute-done((bf16[32,24,128]{2,1,0:T(8,128)(2,1)S(1)}, bf16[32,24,128]{2,1,0:T(8,128)(2,1)S(1)}, u32[]{:S(2)}, u32[]{:S(2)}) %collective-permute-start.3) | collective-permute-done | bytes 196640 | tf_op jit(solution)/shard_map/ppermute | solution.py:363
  41.2 4.4 %shard_map.67 = (bf16[2,5,40,128]{3,2,1,0:T(8,128)(2,1)S(1)}, bf16[2,5,40,128]{3,2,1,0:T(8,128)(2,1)S(1)}, bf16[2,5,40,128]{3,2,1,0:T(8,128)(2,1)S(1)}, bf16[2,5,40,128]{3,2,1,0:T(8,128)(2,1)S(1)}) custom-call(bf16[32,24,128]{2,1,0:T(8,128)(2,1)S(1)} %all_to_all.5.own_ref, bf16[32,24,128]{2,1,0:T(8,128)(2,1)S(1)} %collective-permute-done.3.other_ref), custom_call_target="tpu_custom_call" | custom-call | tf_op jit(solution)/shard_map/pallas_call | solution.py:364
  45.5 0.4 collective-permute-start.4
  45.9 1.7 %collective-permute-start.5 = (bf16[2,5,40,128]{3,2,1,0:T(8,128)(2,1)S(1)}, bf16[2,5,40,128]{3,2,1,0:T(8,128)(2,1)S(1)}, u32[]{:S(2)}, u32[]{:S(2)}) collective-permute-start(bf16[2,5,40,128]{3,2,1,0:T(8,128)(2,1)S(1)} %get-tuple-element.15), channel_id=1, source_target_pairs={{0,128},{4,132},{8,136},{12,140},{16,144},{20,148},{24,152},{28,15... | collective-permute-start | bytes 307208 | tf_op jit(solution)/shard_map/ppermute | solution.py:375
  47.6 1.2 %collective-permute-start.6 = (bf16[2,5,40,128]{3,2,1,0:T(8,128)(2,1)S(1)}, bf16[2,5,40,128]{3,2,1,0:T(8,128)(2,1)S(1)}, u32[]{:S(2)}, u32[]{:S(2)}) collective-permute-start(bf16[2,5,40,128]{3,2,1,0:T(8,128)(2,1)S(1)} %get-tuple-element.16), channel_id=1, source_target_pairs={{0,192},{4,196},{8,200},{12,204},{16,208},{20,212},{24,216},{28,22... | collective-permute-start | bytes 307208 | tf_op jit(solution)/shard_map/ppermute | solution.py:375
  48.8 2.9 %collective-permute-done.4.one_ref = bf16[2,5,40,128]{3,2,1,0:T(8,128)(2,1)S(1)} collective-permute-done((bf16[2,5,40,128]{3,2,1,0:T(8,128)(2,1)S(1)}, bf16[2,5,40,128]{3,2,1,0:T(8,128)(2,1)S(1)}, u32[]{:S(2)}, u32[]{:S(2)}) %collective-permute-start.4) | collective-permute-done | bytes 102432 | tf_op jit(solution)/shard_map/ppermute | solution.py:375
  51.7 0.7 %collective-permute-done.5.two_ref = bf16[2,5,40,128]{3,2,1,0:T(8,128)(2,1)S(1)} collective-permute-done((bf16[2,5,40,128]{3,2,1,0:T(8,128)(2,1)S(1)}, bf16[2,5,40,128]{3,2,1,0:T(8,128)(2,1)S(1)}, u32[]{:S(2)}, u32[]{:S(2)}) %collective-permute-start.5) | collective-permute-done | bytes 102432 | tf_op jit(solution)/shard_map/ppermute | solution.py:375
  52.4 0.9 %collective-permute-done.6.three_ref = bf16[2,5,40,128]{3,2,1,0:T(8,128)(2,1)S(1)} collective-permute-done((bf16[2,5,40,128]{3,2,1,0:T(8,128)(2,1)S(1)}, bf16[2,5,40,128]{3,2,1,0:T(8,128)(2,1)S(1)}, u32[]{:S(2)}, u32[]{:S(2)}) %collective-permute-start.6) | collective-permute-done | bytes 102432 | tf_op jit(solution)/shard_map/ppermute | solution.py:375
  53.4 1.0 %shard_map.68 = bf16[34,40,128]{2,1,0:T(8,128)(2,1)} custom-call(bf16[2,5,40,128]{3,2,1,0:T(8,128)(2,1)S(1)} %get-tuple-element.13.zero_ref, bf16[2,5,40,128]{3,2,1,0:T(8,128)(2,1)S(1)} %collective-permute-done.4.one_ref, bf16[2,5,40,128]{3,2,1,0:T(8,128)(2,1)S(1)} %collective-permute-done.5.two_ref, bf16[2,5,40,128]{3,2,1,0:T(8,128)(2,1)S(1)} %collective-permute-done.6.three_ref), custom_call_target="tpu_custom_call" | custom-call | tf_op jit(solution)/shard_map/pallas_call | solution.py:376
  (7 shorter events, 0.0 us)
Async XLA Ops:
  0.0 9.9 %copy-start.4 = (s32[320]{0:T(512)S(1)}, s32[320]{0:T(512)}, u32[]{:S(2)}) copy-start(s32[320]{0:T(512)} %param.10) | copy-start | bytes 3844
  0.0 9.9 %copy-start.3 = (s32[64]{0:T(128)S(1)}, s32[64]{0:T(128)}, u32[]{:S(2)}) copy-start(s32[64]{0:T(128)} %param.11) | copy-start | bytes 772
  0.0 9.9 %copy-start.2 = (bf16[320,54]{0,1:T(8,128)(2,1)S(1)}, bf16[320,54]{0,1:T(8,128)(2,1)}, u32[]{:S(2)}) copy-start(bf16[320,54]{0,1:T(8,128)(2,1)} %param.9) | copy-start | bytes 103684
  0.0 9.9 %copy-start.1 = (s32[320,54]{0,1:T(8,128)S(1)}, s32[320,54]{0,1:T(8,128)}, u32[]{:S(2)}) copy-start(s32[320,54]{0,1:T(8,128)} %param.8) | copy-start | bytes 207364
  4.7 5.5 %collective-permute-start.2 = (f32[56,320]{1,0:T(8,128)}, f32[56,320]{1,0:T(8,128)S(1)}, u32[]{:S(2)}, u32[]{:S(2)}) collective-permute-start(f32[56,320]{1,0:T(8,128)} %shard_map.64.own_ref), channel_id=1, source_target_pairs={{0,3},{1,0},{2,1},{3,2},{4,7},{5,4},{6,5},{7,6},{8,11},{9,8},{10,9... | collective-permute-start | bytes 215048 | tf_op jit(solution)/shard_map/ppermute | solution.py:346
  8.3 5.9 %collective-permute-start.1 = (f32[56,320]{1,0:T(8,128)}, f32[56,320]{1,0:T(8,128)S(1)}, u32[]{:S(2)}, u32[]{:S(2)}) collective-permute-start(f32[56,320]{1,0:T(8,128)} %shard_map.64.own_ref), channel_id=1, source_target_pairs={{0,1},{1,2},{2,3},{3,0},{4,5},{5,6},{6,7},{7,4},{8,9},{9,10},{10,1... | collective-permute-start | bytes 215048 | tf_op jit(solution)/shard_map/ppermute | solution.py:346
  8.3 5.9 %collective-permute-start = (f32[56,320]{1,0:T(8,128)}, f32[56,320]{1,0:T(8,128)S(1)}, u32[]{:S(2)}, u32[]{:S(2)}) collective-permute-start(f32[56,320]{1,0:T(8,128)} %shard_map.64.own_ref), channel_id=1, source_target_pairs={{0,2},{1,3},{2,0},{3,1},{4,6},{5,7},{6,4},{7,5},{8,10},{9,11},{10,... | collective-permute-start | bytes 215048 | tf_op jit(solution)/shard_map/ppermute | solution.py:346
  14.2 0.9 %copy-start = (f32[56,320]{1,0:T(8,128)S(1)}, f32[56,320]{1,0:T(8,128)}, u32[]{:S(2)}) copy-start(f32[56,320]{1,0:T(8,128)} %shard_map.64.own_ref) | copy-start | bytes 215044
  36.1 5.1 %collective-permute-start.3 = (bf16[32,24,128]{2,1,0:T(8,128)(2,1)S(1)}, bf16[32,24,128]{2,1,0:T(8,128)(2,1)S(1)}, u32[]{:S(2)}, u32[]{:S(2)}) collective-permute-start(bf16[32,24,128]{2,1,0:T(8,128)(2,1)S(1)} %all_to_all.5.own_ref), channel_id=1, source_target_pairs={{0,4},{4,0},{8,12},{12,8},{16,20},{20,16},{24,28},{28,24},{32,36},... | collective-permute-start | bytes 589832 | tf_op jit(solution)/shard_map/ppermute | solution.py:363
  45.5 6.2 %collective-permute-start.4 = (bf16[2,5,40,128]{3,2,1,0:T(8,128)(2,1)S(1)}, bf16[2,5,40,128]{3,2,1,0:T(8,128)(2,1)S(1)}, u32[]{:S(2)}, u32[]{:S(2)}) collective-permute-start(bf16[2,5,40,128]{3,2,1,0:T(8,128)(2,1)S(1)} %get-tuple-element.14), channel_id=1, source_target_pairs={{0,64},{4,68},{8,72},{12,76},{16,80},{20,84},{24,88},{28,92},{32,9... | collective-permute-start | bytes 307208 | tf_op jit(solution)/shard_map/ppermute | solution.py:375
  45.9 6.5 %collective-permute-start.5 = (bf16[2,5,40,128]{3,2,1,0:T(8,128)(2,1)S(1)}, bf16[2,5,40,128]{3,2,1,0:T(8,128)(2,1)S(1)}, u32[]{:S(2)}, u32[]{:S(2)}) collective-permute-start(bf16[2,5,40,128]{3,2,1,0:T(8,128)(2,1)S(1)} %get-tuple-element.15), channel_id=1, source_target_pairs={{0,128},{4,132},{8,136},{12,140},{16,144},{20,148},{24,152},{28,15... | collective-permute-start | bytes 307208 | tf_op jit(solution)/shard_map/ppermute | solution.py:375
  47.6 5.8 %collective-permute-start.6 = (bf16[2,5,40,128]{3,2,1,0:T(8,128)(2,1)S(1)}, bf16[2,5,40,128]{3,2,1,0:T(8,128)(2,1)S(1)}, u32[]{:S(2)}, u32[]{:S(2)}) collective-permute-start(bf16[2,5,40,128]{3,2,1,0:T(8,128)(2,1)S(1)} %get-tuple-element.16), channel_id=1, source_target_pairs={{0,192},{4,196},{8,200},{12,204},{16,208},{20,212},{24,216},{28,22... | collective-permute-start | bytes 307208 | tf_op jit(solution)/shard_map/ppermute | solution.py:375

commit v3 on v2

--- a/solution.py
+++ b/solution.py
@@ -26,7 +26,7 @@
 SENDERS = XS * ZS
 TILES = 11
 LANES = 128
-DEPTH = CORES * TILES * LANES
+DEPTH = TILES * LANES
 COEFS = 40
 PARTS = 5
 TOGETHER = 8
@@ -65,7 +65,9 @@
     return jnp.floor((values.astype(F32) + 0.5) * (1.0 / divisor))
 
 
-def contract_kernel(jac_hbm, dep_ref, out_ref, jac_ref, wide_ref, semaphores):
+def contract_kernel(jac_hbm, dep_hbm, out_ref, jac_ref, dep_ref, wide_ref, semaphores):
+    departures = pltpu.make_async_copy(dep_hbm, dep_ref, semaphores.at[len(PIECES)])
+    departures.start()
     copies = [
         pltpu.make_async_copy(
             jac_hbm.at[pl.ds(start, size)], jac_ref.at[pl.ds(start, size)], semaphores.at[p]
@@ -91,6 +93,7 @@
         ],
         axis=0,
     ).astype(BF16)
+    departures.wait()
     wide_ref[...] = dot_tn(dep_ref[...], spread)
     for copy, (start, size) in zip(copies, PIECES):
         records = slice(start, start + size)
@@ -166,18 +169,16 @@
 
 
 def wave_factors(x, z, core):
-    shape = (88, LANES)
+    shape = (48, LANES)
     row = row_iota(shape)
     lane = lane_iota(shape)
     target = jnp.bitwise_and(row + x, 3)
     first = target * 320 + (core * 20 + z * 40)
-    inner = jnp.maximum(jnp.where(row < 48, row - 8, row - 48), 0)
+    inner = jnp.maximum(row - 8, 0)
     step = lax.shift_right_logical(inner, 1)
     odd = inner - 2 * step
     wave = jnp.where(row < 8, first, step)
-    quarter = jnp.where(
-        row < 4, 0, jnp.where(row < 8, -1, jnp.where(row < 48, odd, odd - 1))
-    ).astype(F32)
+    quarter = jnp.where(row < 4, 0, jnp.where(row < 8, -1, odd)).astype(F32)
     residue = wave.astype(F32) - 84.0 * floor_div(wave, 84)
     lower = jnp.bitwise_and(wave, 63)
     values = jnp.where(
@@ -196,10 +197,7 @@
     return values[:, :16].astype(BF16)
 
 
-def transform_kernel(
-    own_ref, other_ref, out0_ref, out1_ref, out2_ref, out3_ref, block_ref, left_ref, table_ref
-):
-    outs = (out0_ref, out1_ref, out2_ref, out3_ref)
+def transform(arrived_ref, c, block_ref, left_ref, table_ref):
     place = lax.axis_index("band")
     factors = wave_factors(place // 16, lax.rem(place // 2, ZS), lax.rem(place, 2))
     lanes8 = lane_iota((8, LANES))
@@ -208,74 +206,98 @@
     band2 = floor_div(lanes.astype(F32) - GROUP * slot, CAP) * 2.0
     step_rows = row_iota((16, LANES)).astype(F32)
     which = row_iota((16, LANES))
-    for c in range(CORES):
-        left_ref[c, SHARE * 16 :, :] = jnp.zeros((PARTS * LANES - SHARE * 16, DEPTH), BF16)
-
-    for v in range(CORES * TILES):
-        half, tile = v // TILES, v % TILES
-        arrived = (own_ref, other_ref)[half]
+    even = jnp.bitwise_and(row_iota((8, LANES)), 1) == 0
+    left_ref[c, SHARE * 16 :, :] = jnp.zeros((PARTS * LANES - SHARE * 16, DEPTH), BF16)
+
+    for v in range(TILES):
         columns = slice(LANES * v, LANES * (v + 1))
         messages = [
-            arrived[3 * tile + s].astype(F32)
-            if 3 * tile + s < SENDERS
+            arrived_ref[3 * v + s].astype(F32)
+            if 3 * v + s < SENDERS
             else jnp.zeros((24, LANES), F32)
             for s in range(3)
         ]
-        for c in range(CORES):
-            groups = []
-            for s, message in enumerate(messages):
-                near = (GROUP * (s - c)) % LANES
-                far = (GROUP * (s - 2)) % LANES
-                last = pltpu.roll(message[16:24], far, 1)
-                groups.append(
-                    [pltpu.roll(message[8 * t : 8 * t + 8], near, 1) for t in range(3)]
-                    + [
-                        pltpu.roll(message[8 * c : 8 * c + 8], far, 1),
-                        pltpu.roll(last, 4, 0) if c else last,
-                    ]
-                )
-            for t in range(5):
-                block_ref[v, c, t] = jnp.where(
-                    lanes8 < GROUP,
-                    groups[0][t],
-                    jnp.where(
-                        lanes8 < 2 * GROUP,
-                        groups[1][t],
-                        jnp.where(lanes8 < 3 * GROUP, groups[2][t], 0.0),
-                    ),
-                )
-            high = jnp.broadcast_to(block_ref[v, c, 4, 2:3, :], (16, LANES))
-            low = jnp.broadcast_to(block_ref[v, c, 4, 3:4, :], (16, LANES))
-            numbers = jnp.where(
-                which == 0, high, jnp.where(which < 3, low, jnp.where(which == 3, 1.0, 0.0))
+        groups = []
+        for s, message in enumerate(messages):
+            near = (GROUP * (s - c)) % LANES
+            far = (GROUP * (s - 2)) % LANES
+            last = pltpu.roll(message[16:24], far, 1)
+            groups.append(
+                [pltpu.roll(message[8 * t : 8 * t + 8], near, 1) for t in range(3)]
+                + [
+                    pltpu.roll(message[8 * c : 8 * c + 8], far, 1),
+                    pltpu.roll(last, 4, 0) if c else last,
+                ]
+            )
+        for t in range(5):
+            block_ref[v, c, t] = jnp.where(
+                lanes8 < GROUP,
+                groups[0][t],
+                jnp.where(
+                    lanes8 < 2 * GROUP,
+                    groups[1][t],
+                    jnp.where(lanes8 < 3 * GROUP, groups[2][t], 0.0),
+                ),
+            )
+        high = jnp.broadcast_to(block_ref[v, c, 4, 2:3, :], (16, LANES))
+        low = jnp.broadcast_to(block_ref[v, c, 4, 3:4, :], (16, LANES))
+        numbers = jnp.where(
+            which == 0, high, jnp.where(which < 3, low, jnp.where(which == 3, 1.0, 0.0))
+        ).astype(BF16)
+        turns = jnp.dot(factors, numbers, preferred_element_type=F32) * (1.0 / NLON)
+        turns = turns - ((turns + MAGIC) - MAGIC)
+        square = turns * turns
+        series = SIN_TERMS[4]
+        for term in SIN_TERMS[3::-1]:
+            series = series * square + term
+        sine = series * turns
+        waves = 1.0 - 2.0 * (sine * sine)
+        inner_cosine = waves[8:48]
+        inner_sine = jnp.concatenate(
+            [
+                jnp.where(even, -pltpu.roll(part, 7, 0), pltpu.roll(part, 1, 0))
+                for part in (waves[8 + 8 * t : 16 + 8 * t] for t in range(5))
+            ],
+            axis=0,
+        )
+        for pair in range(2):
+            table_ref[c, 80 * pair : 80 * pair + 80, columns] = jnp.concatenate(
+                [
+                    waves[d : d + 1] * inner_cosine - waves[4 + d : 5 + d] * inner_sine
+                    for d in (2 * pair, 2 * pair + 1)
+                ],
+                axis=0,
             ).astype(BF16)
-            turns = jnp.dot(factors, numbers, preferred_element_type=F32) * (1.0 / NLON)
-            turns = turns - ((turns + MAGIC) - MAGIC)
-            square = turns * turns
-            series = SIN_TERMS[4]
-            for term in SIN_TERMS[3::-1]:
-                series = series * square + term
-            sine = series * turns
-            waves = 1.0 - 2.0 * (sine * sine)
-            inner_cosine, inner_sine = waves[8:48], waves[48:88]
-            for pair in range(2):
-                table_ref[c, 80 * pair : 80 * pair + 80, columns] = jnp.concatenate(
-                    [
-                        waves[d : d + 1] * inner_cosine - waves[4 + d : 5 + d] * inner_sine
-                        for d in (2 * pair, 2 * pair + 1)
-                    ],
-                    axis=0,
-                ).astype(BF16)
-            row = band2 + jnp.where(high >= 84.0, 1.0, 0.0)
-            mask = jnp.where(row == step_rows, 1.0, 0.0)
-            for n in range(SHARE):
-                left_ref[c, 16 * n : 16 * n + 16, columns] = (
-                    mask * block_ref[v, c, n // 8, n % 8 : n % 8 + 1, :]
-                ).astype(BF16)
-
+        row = band2 + jnp.where(high >= 84.0, 1.0, 0.0)
+        mask = jnp.where(row == step_rows, 1.0, 0.0)
+        for n in range(SHARE):
+            left_ref[c, 16 * n : 16 * n + 16, columns] = (
+                mask * block_ref[v, c, n // 8, n % 8 : n % 8 + 1, :]
+            ).astype(BF16)
+
+
+SPANS = ((0, 256), (256, 256), (512, 128))
+
+
+def transform_own_kernel(own_ref, sum_ref, block_ref, left_ref, table_ref):
     for c in range(CORES):
-        for start, size in ((0, 256), (256, 256), (512, 128)):
-            result = dot_nt(table_ref[c], left_ref[c, start : start + size, :])
+        transform(own_ref, c, block_ref, left_ref, table_ref)
+        for start, size in SPANS:
+            sum_ref[c, :, start : start + size] = dot_nt(
+                table_ref[c], left_ref[c, start : start + size, :]
+            )
+
+
+def transform_other_kernel(
+    other_ref, sum_ref, out0_ref, out1_ref, out2_ref, out3_ref, block_ref, left_ref, table_ref
+):
+    outs = (out0_ref, out1_ref, out2_ref, out3_ref)
+    for c in range(CORES):
+        transform(other_ref, c, block_ref, left_ref, table_ref)
+        for start, size in SPANS:
+            result = sum_ref[c, :, start : start + size] + dot_nt(
+                table_ref[c], left_ref[c, start : start + size, :]
+            )
             for part in range(size // LANES):
                 for k in range(XS):
                     group = (2 * (-k % XS) + c) % GROUPS
@@ -296,12 +318,14 @@
         values = [sources[g // 2][g % 2, part].astype(F32) for g in range(GROUPS)]
         first = part * TOGETHER
         count = min(TOGETHER, SHARE - first)
+        for bit in (4, 2, 1):
+            low = jnp.bitwise_and(slot, bit) == 0
+            values = [
+                jnp.where(low, values[r], values[(r + bit) % TOGETHER]) for r in range(TOGETHER)
+            ]
         for q in range(count):
-            merged = values[(-q) % TOGETHER]
-            for p in range(1, TOGETHER):
-                merged = jnp.where(slot == p, values[(p - q) % TOGETHER], merged)
             turn = lax.rem(shift + (LANES - 16 * q), LANES)
-            out_ref[first + q] = pltpu.roll(merged, turn, 1).astype(BF16)
+            out_ref[first + q] = pltpu.roll(values[-q % TOGETHER], turn, 1).astype(BF16)
         copy = pltpu.make_async_copy(
             out_ref.at[pl.ds(first, count)], out_hbm.at[pl.ds(first, count)], semaphores.at[part]
         )
@@ -335,11 +359,12 @@
         jax.ShapeDtypeStruct((KP, RECS), F32),
         [
             pltpu.VMEM((RECS, WIDTH), BF16),
+            pltpu.VMEM((CHANNELS, RECS), BF16),
             pltpu.VMEM((RECS, WIDTH), F32),
-            pltpu.SemaphoreType.DMA((len(PIECES),)),
+            pltpu.SemaphoreType.DMA((len(PIECES) + 1,)),
         ],
-        limit=59,
-        in_specs=[hbm, vmem],
+        limit=53,
+        in_specs=[hbm, hbm],
         out_specs=vmem,
     )(jacobian, departures.T)
     others = [
@@ -361,15 +386,21 @@
         packed, "band", split_axis=0, concat_axis=0, axis_index_groups=same_core, tiled=True
     )
     other = lax.ppermute(arrived, "band", [(i, i ^ 1) for i in range(BANDS)])
+    scratch = [
+        pltpu.VMEM((TILES, CORES, 5, 8, LANES), F32),
+        pltpu.VMEM((CORES, PARTS * LANES, DEPTH), BF16),
+        pltpu.VMEM((CORES, XS * COEFS, DEPTH), BF16),
+    ]
+    own_sum = call(
+        transform_own_kernel,
+        jax.ShapeDtypeStruct((CORES, XS * COEFS, PARTS * LANES), F32),
+        scratch,
+    )(arrived)
     spectra = call(
-        transform_kernel,
+        transform_other_kernel,
         [jax.ShapeDtypeStruct((CORES, PARTS, COEFS, LANES), BF16)] * XS,
-        [
-            pltpu.VMEM((CORES * TILES, CORES, 5, 8, LANES), F32),
-            pltpu.VMEM((CORES, PARTS * LANES, DEPTH), BF16),
-            pltpu.VMEM((CORES, XS * COEFS, DEPTH), BF16),
-        ],
-    )(arrived, other)
+        scratch,
+    )(other, own_sum)
     received = [spectra[0]] + [None] * 3
     for k in (2, 1, 3):
         received[k] = lax.ppermute(spectra[k], "band", x_shift(k))

time: 54.5 us -> 52 us (0.954)
  Pallas kernels: 10.9 us -> 9.3 us
  waiting for transfers between devices: 9.7 us -> 8.85 us
    pallas_call x1, Pallas kernels: 4.63 us -> 3.18 us  [local(): call(contract_kernel, jax.ShapeDtypeStruct((KP, RECS), F32), [pltpu.VMEM(...]
    ppermute x1, waiting for transfers between devices: 1.07 us -> 0.01 us  [local(): other = lax.ppermute(arrived, 'band', [(i, i ^ 1) for i in range(BANDS)])]
    pallas_call x1 -> x2, Pallas kernels: 4.36 us -> 4.3 us  [the longest x1 2.19 us: local(): call(transform_other_kernel, [jax.ShapeDtypeStruct((CORES, PARTS, COEFS,...]
  transfers between devices with their start and end apart: 7 -> 7, of which waited for: 5 -> 3; matrix products, arithmetic and copies ran while one was open for 0% -> 0% of each run, Pallas kernels for 0% -> 4%
where the time goes in v3:
time: 52 us; the launch traced here: 51.8 us
  blocking collectives  20.2 us (39%)
  starting transfers between devices  12.6 us (24%)
  Pallas kernels  9.3 us (18%)
  waiting for transfers between devices  8.85 us (17%)
  local copies, waits for them, and re-layouts  0.85 us (2%)
    all_to_all x1, blocking collectives, local(): lax.all_to_all(packed, 'band', split_axis=0, concat_axis=0, axis_index_gr...  20.2 us
    ppermute x3, starting transfers between devices, local(): lax.ppermute(partial, 'lev', [(i, (i + k) % 4) for i in range(4)])  5.29 us
    ppermute x3, waiting for transfers between devices, local(): received[k] = lax.ppermute(spectra[k], 'band', x_shift(k))  4.97 us
    ppermute x1, starting transfers between devices, local(): other = lax.ppermute(arrived, 'band', [(i, i ^ 1) for i in range(BANDS)])  3.99 us
    ppermute x3, waiting for transfers between devices, local(): lax.ppermute(partial, 'lev', [(i, (i + k) % 4) for i in range(4)])  3.87 us
    ppermute x3, starting transfers between devices, local(): received[k] = lax.ppermute(spectra[k], 'band', x_shift(k))  3.28 us
    pallas_call x1, Pallas kernels, local(): call(contract_kernel, jax.ShapeDtypeStruct((KP, RECS), F32), [pltpu.VMEM(...  3.18 us
    pallas_call x1, Pallas kernels, local(): call(transform_other_kernel, [jax.ShapeDtypeStruct((CORES, PARTS, COEFS,...  2.19 us
  transfers between devices with their start and end apart: 7, of which 3 were waited for; matrix products, arithmetic and copies ran while one was open for 0% of the time, Pallas kernels for 4%

profile of v3, /device:TPU:1, one launch (start us, length us, event | category | flops | bytes accessed | tf_op | source)
XLA Modules:
  0.0 51.8 jit_solution(13927738873533073541)
XLA Ops:
  0.0 0.8 %copy-done.1 = bf16[320,64]{0,1:T(8,128)(2,1)S(1)} copy-done((bf16[320,64]{0,1:T(8,128)(2,1)S(1)}, bf16[320,64]{0,1:T(8,128)(2,1)}, u32[]{:S(2)}) %copy-start.1) | copy-done | bytes 40984
  0.8 3.2 %shard_map.64.own_ref = f32[56,320]{1,0:T(8,128)S(1)} custom-call(bf16[320,3456]{1,0:T(8,128)(2,1)} %jac_hbm.1, bf16[64,320]{1,0:T(8,128)(2,1)S(1)} %bitcast.6), custom_call_target="tpu_custom_call" | custom-call | tf_op jit(solution)/shard_map/pallas_call | solution.py:357
  4.0 3.6 %collective-permute-start.2 = (f32[56,320]{1,0:T(8,128)S(1)}, f32[56,320]{1,0:T(8,128)S(1)}, u32[]{:S(2)}, u32[]{:S(2)}) collective-permute-start(f32[56,320]{1,0:T(8,128)S(1)} %shard_map.64.own_ref), channel_id=1, source_target_pairs={{0,3},{1,0},{2,1},{3,2},{4,7},{5,4},{6,5},{7,6},{8,11},{9,8},{10,9... | collective-permute-start | bytes 215048 | tf_op jit(solution)/shard_map/ppermute | solution.py:371
  7.7 0.0 collective-permute-start.1
  7.7 1.6 %collective-permute-start = (f32[56,320]{1,0:T(8,128)S(1)}, f32[56,320]{1,0:T(8,128)S(1)}, u32[]{:S(2)}, u32[]{:S(2)}) collective-permute-start(f32[56,320]{1,0:T(8,128)S(1)} %shard_map.64.own_ref), channel_id=1, source_target_pairs={{0,2},{1,3},{2,0},{3,1},{4,6},{5,7},{6,4},{7,5},{8,10},{9,11},{10,... | collective-permute-start | bytes 215048 | tf_op jit(solution)/shard_map/ppermute | solution.py:371
  9.3 0.0 copy-done.4
  9.3 0.0 copy-done
  9.4 0.1 shard_map.65
  9.5 0.0 collective-permute-done.2.three_ref
  9.5 3.8 %collective-permute-done.1.two_ref = f32[56,320]{1,0:T(8,128)S(1)} collective-permute-done((f32[56,320]{1,0:T(8,128)S(1)}, f32[56,320]{1,0:T(8,128)S(1)}, u32[]{:S(2)}, u32[]{:S(2)}) %collective-permute-start.1) | collective-permute-done | bytes 71712 | tf_op jit(solution)/shard_map/ppermute | solution.py:371
  13.3 0.0 collective-permute-done.one_ref
  13.4 0.8 %shard_map.66 = bf16[32,24,128]{2,1,0:T(8,128)(2,1)S(1)} custom-call(f32[56,320]{1,0:T(8,128)S(1)} %shard_map.64.own_ref, f32[56,320]{1,0:T(8,128)S(1)} %collective-permute-done.one_ref, f32[56,320]{1,0:T(8,128)S(1)} %collective-permute-done.1.two_ref, f32[56,320]{1,0:T(8,128)S(1)} %collective-permute-done.2.three_ref, ...), custom_call_target="tpu_custom_call" | custom-call | tf_op jit(solution)/shard_map/pallas_call | solution.py:377
  14.1 20.2 %all_to_all.5.own_ref = bf16[32,24,128]{2,1,0:T(8,128)(2,1)S(1)} all-to-all(bf16[32,24,128]{2,1,0:T(8,128)(2,1)S(1)} %shard_map.66), channel_id=1, replica_groups={{0,8,16,24,32,40,48,56,64,72,80,88,96,104,112,120,128,136,144,152,160,1..., dimensions={0} | all-to-all | bytes 393216 | tf_op jit(solution)/shard_map/all_to_all | solution.py:385
  34.4 4.0 %collective-permute-start.3 = (bf16[32,24,128]{2,1,0:T(8,128)(2,1)S(1)}, bf16[32,24,128]{2,1,0:T(8,128)(2,1)S(1)}, u32[]{:S(2)}, u32[]{:S(2)}) collective-permute-start(bf16[32,24,128]{2,1,0:T(8,128)(2,1)S(1)} %all_to_all.5.own_ref), channel_id=1, source_target_pairs={{0,4},{4,0},{8,12},{12,8},{16,20},{20,16},{24,28},{28,24},{32,36},... | collective-permute-start | bytes 589832 | tf_op jit(solution)/shard_map/ppermute | solution.py:388
  38.4 2.1 %shard_map.67.sum_ref = f32[2,160,640]{2,1,0:T(8,128)S(1)} custom-call(bf16[32,24,128]{2,1,0:T(8,128)(2,1)S(1)} %all_to_all.5.own_ref), custom_call_target="tpu_custom_call" | custom-call | tf_op jit(solution)/shard_map/pallas_call | solution.py:394
  40.5 0.0 collective-permute-done.3.other_ref
  40.5 2.2 %shard_map.68 = (bf16[2,5,40,128]{3,2,1,0:T(8,128)(2,1)S(1)}, bf16[2,5,40,128]{3,2,1,0:T(8,128)(2,1)S(1)}, bf16[2,5,40,128]{3,2,1,0:T(8,128)(2,1)S(1)}, bf16[2,5,40,128]{3,2,1,0:T(8,128)(2,1)S(1)}) custom-call(bf16[32,24,128]{2,1,0:T(8,128)(2,1)S(1)} %collective-permute-done.3.other_ref, f32[2,160,640]{2,1,0:T(8,128)S(1)} %shard_map.67.sum_ref), custom_call_target="tpu_custom_call" | custom-call | tf_op jit(solution)/shard_map/pallas_call | solution.py:399
  42.7 0.4 collective-permute-start.4
  43.1 1.7 %collective-permute-start.5 = (bf16[2,5,40,128]{3,2,1,0:T(8,128)(2,1)S(1)}, bf16[2,5,40,128]{3,2,1,0:T(8,128)(2,1)S(1)}, u32[]{:S(2)}, u32[]{:S(2)}) collective-permute-start(bf16[2,5,40,128]{3,2,1,0:T(8,128)(2,1)S(1)} %get-tuple-element.15), channel_id=1, source_target_pairs={{0,128},{4,132},{8,136},{12,140},{16,144},{20,148},{24,152},{28,15... | collective-permute-start | bytes 307208 | tf_op jit(solution)/shard_map/ppermute | solution.py:406
  44.8 1.2 %collective-permute-start.6 = (bf16[2,5,40,128]{3,2,1,0:T(8,128)(2,1)S(1)}, bf16[2,5,40,128]{3,2,1,0:T(8,128)(2,1)S(1)}, u32[]{:S(2)}, u32[]{:S(2)}) collective-permute-start(bf16[2,5,40,128]{3,2,1,0:T(8,128)(2,1)S(1)} %get-tuple-element.16), channel_id=1, source_target_pairs={{0,192},{4,196},{8,200},{12,204},{16,208},{20,212},{24,216},{28,22... | collective-permute-start | bytes 307208 | tf_op jit(solution)/shard_map/ppermute | solution.py:406
  46.0 4.7 %collective-permute-done.4.one_ref = bf16[2,5,40,128]{3,2,1,0:T(8,128)(2,1)S(1)} collective-permute-done((bf16[2,5,40,128]{3,2,1,0:T(8,128)(2,1)S(1)}, bf16[2,5,40,128]{3,2,1,0:T(8,128)(2,1)S(1)}, u32[]{:S(2)}, u32[]{:S(2)}) %collective-permute-start.4) | collective-permute-done | bytes 102432 | tf_op jit(solution)/shard_map/ppermute | solution.py:406
  50.7 0.0 collective-permute-done.5.two_ref
  50.7 0.3 collective-permute-done.6.three_ref
  50.9 0.9 %shard_map.69 = bf16[34,40,128]{2,1,0:T(8,128)(2,1)} custom-call(bf16[2,5,40,128]{3,2,1,0:T(8,128)(2,1)S(1)} %get-tuple-element.13.zero_ref, bf16[2,5,40,128]{3,2,1,0:T(8,128)(2,1)S(1)} %collective-permute-done.4.one_ref, bf16[2,5,40,128]{3,2,1,0:T(8,128)(2,1)S(1)} %collective-permute-done.5.two_ref, bf16[2,5,40,128]{3,2,1,0:T(8,128)(2,1)S(1)} %collective-permute-done.6.three_ref), custom_call_target="tpu_custom_call" | custom-call | tf_op jit(solution)/shard_map/pallas_call | solution.py:407
  (8 shorter events, 0.0 us)
Async XLA Ops:
  0.0 9.3 %copy-start = (s32[320,54]{0,1:T(8,128)S(1)}, s32[320,54]{0,1:T(8,128)}, u32[]{:S(2)}) copy-start(s32[320,54]{0,1:T(8,128)} %param.8) | copy-start | bytes 207364
  0.0 0.8 %copy-start.1 = (bf16[320,64]{0,1:T(8,128)(2,1)S(1)}, bf16[320,64]{0,1:T(8,128)(2,1)}, u32[]{:S(2)}) copy-start(bf16[320,64]{0,1:T(8,128)(2,1)} %param.7) | copy-start | bytes 122884
  0.8 8.5 %copy-start.4 = (s32[320]{0:T(512)S(1)}, s32[320]{0:T(512)}, u32[]{:S(2)}) copy-start(s32[320]{0:T(512)} %param.10) | copy-start | bytes 3844
  0.8 8.5 %copy-start.2 = (bf16[320,54]{0,1:T(8,128)(2,1)S(1)}, bf16[320,54]{0,1:T(8,128)(2,1)}, u32[]{:S(2)}) copy-start(bf16[320,54]{0,1:T(8,128)(2,1)} %param.9) | copy-start | bytes 103684
  0.8 8.5 %copy-start.3 = (s32[64]{0:T(128)S(1)}, s32[64]{0:T(128)}, u32[]{:S(2)}) copy-start(s32[64]{0:T(128)} %param.11) | copy-start | bytes 772
  4.0 5.5 %collective-permute-start.2 = (f32[56,320]{1,0:T(8,128)S(1)}, f32[56,320]{1,0:T(8,128)S(1)}, u32[]{:S(2)}, u32[]{:S(2)}) collective-permute-start(f32[56,320]{1,0:T(8,128)S(1)} %shard_map.64.own_ref), channel_id=1, source_target_pairs={{0,3},{1,0},{2,1},{3,2},{4,7},{5,4},{6,5},{7,6},{8,11},{9,8},{10,9... | collective-permute-start | bytes 215048 | tf_op jit(solution)/shard_map/ppermute | solution.py:371
  7.7 5.6 %collective-permute-start.1 = (f32[56,320]{1,0:T(8,128)S(1)}, f32[56,320]{1,0:T(8,128)S(1)}, u32[]{:S(2)}, u32[]{:S(2)}) collective-permute-start(f32[56,320]{1,0:T(8,128)S(1)} %shard_map.64.own_ref), channel_id=1, source_target_pairs={{0,1},{1,2},{2,3},{3,0},{4,5},{5,6},{6,7},{7,4},{8,9},{9,10},{10,1... | collective-permute-start | bytes 215048 | tf_op jit(solution)/shard_map/ppermute | solution.py:371
  7.7 5.7 %collective-permute-start = (f32[56,320]{1,0:T(8,128)S(1)}, f32[56,320]{1,0:T(8,128)S(1)}, u32[]{:S(2)}, u32[]{:S(2)}) collective-permute-start(f32[56,320]{1,0:T(8,128)S(1)} %shard_map.64.own_ref), channel_id=1, source_target_pairs={{0,2},{1,3},{2,0},{3,1},{4,6},{5,7},{6,4},{7,5},{8,10},{9,11},{10,... | collective-permute-start | bytes 215048 | tf_op jit(solution)/shard_map/ppermute | solution.py:371
  34.4 6.1 %collective-permute-start.3 = (bf16[32,24,128]{2,1,0:T(8,128)(2,1)S(1)}, bf16[32,24,128]{2,1,0:T(8,128)(2,1)S(1)}, u32[]{:S(2)}, u32[]{:S(2)}) collective-permute-start(bf16[32,24,128]{2,1,0:T(8,128)(2,1)S(1)} %all_to_all.5.own_ref), channel_id=1, source_target_pairs={{0,4},{4,0},{8,12},{12,8},{16,20},{20,16},{24,28},{28,24},{32,36},... | collective-permute-start | bytes 589832 | tf_op jit(solution)/shard_map/ppermute | solution.py:388
  42.7 8.0 %collective-permute-start.4 = (bf16[2,5,40,128]{3,2,1,0:T(8,128)(2,1)S(1)}, bf16[2,5,40,128]{3,2,1,0:T(8,128)(2,1)S(1)}, u32[]{:S(2)}, u32[]{:S(2)}) collective-permute-start(bf16[2,5,40,128]{3,2,1,0:T(8,128)(2,1)S(1)} %get-tuple-element.14), channel_id=1, source_target_pairs={{0,64},{4,68},{8,72},{12,76},{16,80},{20,84},{24,88},{28,92},{32,9... | collective-permute-start | bytes 307208 | tf_op jit(solution)/shard_map/ppermute | solution.py:406
  43.1 7.6 %collective-permute-start.5 = (bf16[2,5,40,128]{3,2,1,0:T(8,128)(2,1)S(1)}, bf16[2,5,40,128]{3,2,1,0:T(8,128)(2,1)S(1)}, u32[]{:S(2)}, u32[]{:S(2)}) collective-permute-start(bf16[2,5,40,128]{3,2,1,0:T(8,128)(2,1)S(1)} %get-tuple-element.15), channel_id=1, source_target_pairs={{0,128},{4,132},{8,136},{12,140},{16,144},{20,148},{24,152},{28,15... | collective-permute-start | bytes 307208 | tf_op jit(solution)/shard_map/ppermute | solution.py:406
  44.8 6.2 %collective-permute-start.6 = (bf16[2,5,40,128]{3,2,1,0:T(8,128)(2,1)S(1)}, bf16[2,5,40,128]{3,2,1,0:T(8,128)(2,1)S(1)}, u32[]{:S(2)}, u32[]{:S(2)}) collective-permute-start(bf16[2,5,40,128]{3,2,1,0:T(8,128)(2,1)S(1)} %get-tuple-element.16), channel_id=1, source_target_pairs={{0,192},{4,196},{8,200},{12,204},{16,208},{20,212},{24,216},{28,22... | collective-permute-start | bytes 307208 | tf_op jit(solution)/shard_map/ppermute | solution.py:406

commit v4 on v3

--- a/solution.py
+++ b/solution.py
@@ -1,3 +1,4 @@
+import functools
 import math
 
 import jax
@@ -24,7 +25,7 @@
 CORES = 2
 BANDS = 64
 SENDERS = XS * ZS
-TILES = 11
+TILES = 10
 LANES = 128
 DEPTH = TILES * LANES
 COEFS = 40
@@ -65,40 +66,33 @@
     return jnp.floor((values.astype(F32) + 0.5) * (1.0 / divisor))
 
 
-def contract_kernel(jac_hbm, dep_hbm, out_ref, jac_ref, dep_ref, wide_ref, semaphores):
-    departures = pltpu.make_async_copy(dep_hbm, dep_ref, semaphores.at[len(PIECES)])
-    departures.start()
-    copies = [
-        pltpu.make_async_copy(
-            jac_hbm.at[pl.ds(start, size)], jac_ref.at[pl.ds(start, size)], semaphores.at[p]
-        )
-        for p, (start, size) in enumerate(PIECES)
-    ]
-    for copy in copies:
-        copy.start()
+def channel_and_level():
     position = lane_iota((8, WIDTH))
     channel = floor_div(position, KL)
-    level = position.astype(F32) - KL * channel
-    spread = jnp.concatenate(
-        [
-            jnp.where(channel == (row_iota((8, WIDTH)) + 8 * t).astype(F32), 1.0, 0.0)
-            for t in range(CHANNELS // 8)
-        ],
+    return channel, position.astype(F32) - KL * channel
+
+
+def chosen(values, count):
+    rows = row_iota((8, values.shape[1]))
+    return jnp.concatenate(
+        [jnp.where(values == (rows + 8 * t).astype(F32), 1.0, 0.0) for t in range(count // 8)],
         axis=0,
     ).astype(BF16)
-    select = jnp.concatenate(
-        [
-            jnp.where(level == (row_iota((8, WIDTH)) + 8 * t).astype(F32), 1.0, 0.0)
-            for t in range(KP // 8)
-        ],
-        axis=0,
-    ).astype(BF16)
-    departures.wait()
-    wide_ref[...] = dot_tn(dep_ref[...], spread)
-    for copy, (start, size) in zip(copies, PIECES):
+
+
+def spread_kernel(dep_ref, wide_ref):
+    channel, _ = channel_and_level()
+    wide_ref[...] = dot_tn(dep_ref[...], chosen(channel, CHANNELS))
+
+
+def contract_kernel(jac_ref, wide_ref, out_ref):
+    _, level = channel_and_level()
+    half = WIDTH // 2
+    select = chosen(level[:, :half], KP)
+    for start, size in PIECES:
         records = slice(start, start + size)
-        copy.wait()
         product = jac_ref[records, :].astype(F32) * wide_ref[records, :]
+        product = product[:, :half] + product[:, half:]
         high = product.astype(BF16)
         low = (product - high.astype(F32)).astype(BF16)
         out_ref[:, records] = dot_nt(select, high) + dot_nt(select, low)
@@ -197,50 +191,40 @@
     return values[:, :16].astype(BF16)
 
 
-def transform(arrived_ref, c, block_ref, left_ref, table_ref):
+def transform(arrived_ref, c, block_ref, left_ref, table_ref, between=()):
     place = lax.axis_index("band")
     factors = wave_factors(place // 16, lax.rem(place // 2, ZS), lax.rem(place, 2))
     lanes8 = lane_iota((8, LANES))
     lanes = lane_iota((16, LANES))
-    slot = floor_div(lanes, GROUP)
-    band2 = floor_div(lanes.astype(F32) - GROUP * slot, CAP) * 2.0
     step_rows = row_iota((16, LANES)).astype(F32)
     which = row_iota((16, LANES))
     even = jnp.bitwise_and(row_iota((8, LANES)), 1) == 0
-    left_ref[c, SHARE * 16 :, :] = jnp.zeros((PARTS * LANES - SHARE * 16, DEPTH), BF16)
+    left_ref[SHARE * 16 :, :] = jnp.zeros((PARTS * LANES - SHARE * 16, DEPTH), BF16)
 
     for v in range(TILES):
         columns = slice(LANES * v, LANES * (v + 1))
-        messages = [
-            arrived_ref[3 * v + s].astype(F32)
-            if 3 * v + s < SENDERS
-            else jnp.zeros((24, LANES), F32)
-            for s in range(3)
-        ]
-        groups = []
-        for s, message in enumerate(messages):
-            near = (GROUP * (s - c)) % LANES
-            far = (GROUP * (s - 2)) % LANES
+        base = LANES * (v % 5)
+        block8 = floor_div(lanes8 + base, GROUP)
+        block16 = floor_div(lanes + base, GROUP)
+        band2 = floor_div((lanes + base).astype(F32) - GROUP * block16, CAP) * 2.0
+        total = None
+        for e in range(base // GROUP, (base + LANES - 1) // GROUP + 1):
+            message = arrived_ref[16 * (v // 5) + e].astype(F32)
+            near = (GROUP * (e - c) - base) % LANES
+            far = (GROUP * (e - 2) - base) % LANES
             last = pltpu.roll(message[16:24], far, 1)
-            groups.append(
-                [pltpu.roll(message[8 * t : 8 * t + 8], near, 1) for t in range(3)]
-                + [
-                    pltpu.roll(message[8 * c : 8 * c + 8], far, 1),
-                    pltpu.roll(last, 4, 0) if c else last,
-                ]
-            )
+            parts = [pltpu.roll(message[8 * t : 8 * t + 8], near, 1) for t in range(3)] + [
+                pltpu.roll(message[8 * c : 8 * c + 8], far, 1),
+                pltpu.roll(last, 4, 0) if c else last,
+            ]
+            if total is None:
+                total = parts
+            else:
+                total = [jnp.where(block8 == e, new, old) for new, old in zip(parts, total)]
         for t in range(5):
-            block_ref[v, c, t] = jnp.where(
-                lanes8 < GROUP,
-                groups[0][t],
-                jnp.where(
-                    lanes8 < 2 * GROUP,
-                    groups[1][t],
-                    jnp.where(lanes8 < 3 * GROUP, groups[2][t], 0.0),
-                ),
-            )
-        high = jnp.broadcast_to(block_ref[v, c, 4, 2:3, :], (16, LANES))
-        low = jnp.broadcast_to(block_ref[v, c, 4, 3:4, :], (16, LANES))
+            block_ref[v, t] = total[t]
+        high = jnp.broadcast_to(block_ref[v, 4, 2:3, :], (16, LANES))
+        low = jnp.broadcast_to(block_ref[v, 4, 3:4, :], (16, LANES))
         numbers = jnp.where(
             which == 0, high, jnp.where(which < 3, low, jnp.where(which == 3, 1.0, 0.0))
         ).astype(BF16)
@@ -261,7 +245,7 @@
             axis=0,
         )
         for pair in range(2):
-            table_ref[c, 80 * pair : 80 * pair + 80, columns] = jnp.concatenate(
+            table_ref[80 * pair : 80 * pair + 80, columns] = jnp.concatenate(
                 [
                     waves[d : d + 1] * inner_cosine - waves[4 + d : 5 + d] * inner_sine
                     for d in (2 * pair, 2 * pair + 1)
@@ -271,42 +255,52 @@
         row = band2 + jnp.where(high >= 84.0, 1.0, 0.0)
         mask = jnp.where(row == step_rows, 1.0, 0.0)
         for n in range(SHARE):
-            left_ref[c, 16 * n : 16 * n + 16, columns] = (
-                mask * block_ref[v, c, n // 8, n % 8 : n % 8 + 1, :]
+            left_ref[16 * n : 16 * n + 16, columns] = (
+                mask * block_ref[v, n // 8, n % 8 : n % 8 + 1, :]
             ).astype(BF16)
+        if v % 3 == 2 and v // 3 < len(between):
+            between[v // 3]()
 
 
 SPANS = ((0, 256), (256, 256), (512, 128))
 
 
-def transform_own_kernel(own_ref, sum_ref, block_ref, left_ref, table_ref):
-    for c in range(CORES):
-        transform(own_ref, c, block_ref, left_ref, table_ref)
-        for start, size in SPANS:
-            sum_ref[c, :, start : start + size] = dot_nt(
-                table_ref[c], left_ref[c, start : start + size, :]
-            )
-
-
-def transform_other_kernel(
-    other_ref, sum_ref, out0_ref, out1_ref, out2_ref, out3_ref, block_ref, left_ref, table_ref
-):
+def transform_own_kernel(own_ref, sum_ref, *scratch):
+    blocks, lefts, tables = scratch[0:2], scratch[2:4], scratch[4:6]
+
+    def multiply(c, start, size):
+        sum_ref[c, :, start : start + size] = dot_nt(
+            tables[c][...], lefts[c][start : start + size, :]
+        )
+
+    transform(own_ref, 0, blocks[0], lefts[0], tables[0])
+    steps = [functools.partial(multiply, 0, *span) for span in SPANS]
+    transform(own_ref, 1, blocks[1], lefts[1], tables[1], steps)
+    for span in SPANS:
+        multiply(1, *span)
+
+
+def transform_other_kernel(other_ref, sum_ref, out0_ref, out1_ref, out2_ref, out3_ref, *scratch):
     outs = (out0_ref, out1_ref, out2_ref, out3_ref)
-    for c in range(CORES):
-        transform(other_ref, c, block_ref, left_ref, table_ref)
-        for start, size in SPANS:
-            result = sum_ref[c, :, start : start + size] + dot_nt(
-                table_ref[c], left_ref[c, start : start + size, :]
-            )
-            for part in range(size // LANES):
-                for k in range(XS):
-                    group = (2 * (-k % XS) + c) % GROUPS
-                    piece = result[
-                        COEFS * k : COEFS * (k + 1), LANES * part : LANES * (part + 1)
-                    ]
-                    if group:
-                        piece = pltpu.roll(piece, 16 * group, 1)
-                    outs[k][c, start // LANES + part] = piece.astype(BF16)
+    blocks, lefts, tables = scratch[0:2], scratch[2:4], scratch[4:6]
+
+    def multiply(c, start, size):
+        result = sum_ref[c, :, start : start + size] + dot_nt(
+            tables[c][...], lefts[c][start : start + size, :]
+        )
+        for part in range(size // LANES):
+            for k in range(XS):
+                group = (2 * (-k % XS) + c) % GROUPS
+                piece = result[COEFS * k : COEFS * (k + 1), LANES * part : LANES * (part + 1)]
+                if group:
+                    piece = pltpu.roll(piece, 16 * group, 1)
+                outs[k][c, start // LANES + part] = piece.astype(BF16)
+
+    transform(other_ref, 0, blocks[0], lefts[0], tables[0])
+    steps = [functools.partial(multiply, 0, *span) for span in SPANS]
+    transform(other_ref, 1, blocks[1], lefts[1], tables[1], steps)
+    for span in SPANS:
+        multiply(1, *span)
 
 
 def place_kernel(zero_ref, one_ref, two_ref, three_ref, out_hbm, out_ref, semaphores):
@@ -354,19 +348,8 @@
 def local(jacobian, departures, level_index, level_weight, column_index, record_counts):
     vmem = pl.BlockSpec(memory_space=pltpu.VMEM)
     hbm = pl.BlockSpec(memory_space=pltpu.HBM)
-    partial = call(
-        contract_kernel,
-        jax.ShapeDtypeStruct((KP, RECS), F32),
-        [
-            pltpu.VMEM((RECS, WIDTH), BF16),
-            pltpu.VMEM((CHANNELS, RECS), BF16),
-            pltpu.VMEM((RECS, WIDTH), F32),
-            pltpu.SemaphoreType.DMA((len(PIECES) + 1,)),
-        ],
-        limit=53,
-        in_specs=[hbm, hbm],
-        out_specs=vmem,
-    )(jacobian, departures.T)
+    wide = call(spread_kernel, jax.ShapeDtypeStruct((RECS, WIDTH), F32))(departures.T)
+    partial = call(contract_kernel, jax.ShapeDtypeStruct((KP, RECS), F32))(jacobian, wide)
     others = [
         lax.ppermute(partial, "lev", [(i, (i + k) % 4) for i in range(4)]) for k in (2, 1, 3)
     ]
@@ -386,11 +369,11 @@
         packed, "band", split_axis=0, concat_axis=0, axis_index_groups=same_core, tiled=True
     )
     other = lax.ppermute(arrived, "band", [(i, i ^ 1) for i in range(BANDS)])
-    scratch = [
-        pltpu.VMEM((TILES, CORES, 5, 8, LANES), F32),
-        pltpu.VMEM((CORES, PARTS * LANES, DEPTH), BF16),
-        pltpu.VMEM((CORES, XS * COEFS, DEPTH), BF16),
-    ]
+    scratch = (
+        [pltpu.VMEM((TILES, 5, 8, LANES), F32)] * CORES
+        + [pltpu.VMEM((PARTS * LANES, DEPTH), BF16)] * CORES
+        + [pltpu.VMEM((XS * COEFS, DEPTH), BF16)] * CORES
+    )
     own_sum = call(
         transform_own_kernel,
         jax.ShapeDtypeStruct((CORES, XS * COEFS, PARTS * LANES), F32),

time: 52 us -> 49.4 us (0.950)
  Pallas kernels: 9.3 us -> 7.76 us
  blocking collectives: 20.2 us -> 18.7 us
  starting transfers between devices: 12.6 us -> 13.6 us
  waiting for transfers between devices: 8.85 us -> 8.22 us
    all_to_all x1, blocking collectives: 20.2 us -> 18.7 us  [local(): lax.all_to_all(packed, 'band', split_axis=0, concat_axis=0, axis_index_gr...]
    ppermute x3, starting transfers between devices: 5.29 us -> 6.51 us  [local(): lax.ppermute(partial, 'lev', [(i, (i + k) % 4) for i in range(4)])]
    pallas_call x1 -> x2, Pallas kernels: 3.18 us -> 2 us  [the longest x1 1.23 us: local(): call(contract_kernel, jax.ShapeDtypeStruct((KP, RECS), F32))(jacobian, wide)]
    ppermute x3, waiting for transfers between devices: 3.87 us -> 3.29 us  [local(): lax.ppermute(partial, 'lev', [(i, (i + k) % 4) for i in range(4)])]
where the time goes in v4:
time: 49.4 us; the launch traced here: 49.3 us
  blocking collectives  18.7 us (38%)
  starting transfers between devices  13.6 us (28%)
  waiting for transfers between devices  8.22 us (17%)
  Pallas kernels  7.76 us (16%)
  local copies, waits for them, and re-layouts  0.98 us (2%)
    all_to_all x1, blocking collectives, local(): lax.all_to_all(packed, 'band', split_axis=0, concat_axis=0, axis_index_gr...  18.7 us
    ppermute x3, starting transfers between devices, local(): lax.ppermute(partial, 'lev', [(i, (i + k) % 4) for i in range(4)])  6.51 us
    ppermute x3, waiting for transfers between devices, local(): received[k] = lax.ppermute(spectra[k], 'band', x_shift(k))  4.92 us
    ppermute x1, starting transfers between devices, local(): other = lax.ppermute(arrived, 'band', [(i, i ^ 1) for i in range(BANDS)])  3.79 us
    ppermute x3, starting transfers between devices, local(): received[k] = lax.ppermute(spectra[k], 'band', x_shift(k))  3.32 us
    ppermute x3, waiting for transfers between devices, local(): lax.ppermute(partial, 'lev', [(i, (i + k) % 4) for i in range(4)])  3.29 us
    pallas_call x1, Pallas kernels, local(): call(transform_other_kernel, [jax.ShapeDtypeStruct((CORES, PARTS, COEFS,...  1.99 us
    pallas_call x1, Pallas kernels, local(): call(transform_own_kernel, jax.ShapeDtypeStruct((CORES, XS * COEFS, PARTS...  1.96 us
  transfers between devices with their start and end apart: 7, of which 3 were waited for; matrix products, arithmetic and copies ran while one was open for 0% of the time, Pallas kernels for 4%

profile of v4, /device:TPU:1, one launch (start us, length us, event | category | flops | bytes accessed | tf_op | source)
XLA Modules:
  0.0 49.3 jit_solution(7149281248612311901)
XLA Ops:
  0.0 0.9 %copy-done.2 = bf16[320,64]{0,1:T(8,128)(2,1)S(1)} copy-done((bf16[320,64]{0,1:T(8,128)(2,1)S(1)}, bf16[320,64]{0,1:T(8,128)(2,1)}, u32[]{:S(2)}) %copy-start.2) | copy-done | bytes 40984
  1.0 0.8 %shard_map.64.wide_ref = f32[320,3456]{1,0:T(8,128)S(1)} custom-call(bf16[64,320]{1,0:T(8,128)(2,1)S(1)} %bitcast.6), custom_call_target="tpu_custom_call" | custom-call | tf_op jit(solution)/shard_map/pallas_call | solution.py:351
  1.7 0.0 copy-start.5
  1.7 0.0 copy-start.1
  1.8 0.0 copy-start.3
  1.8 0.0 copy-start.4
  1.8 1.2 %shard_map.65.own_ref = f32[56,320]{1,0:T(8,128)S(1)} custom-call(bf16[320,3456]{1,0:T(8,128)(2,1)S(1)} %copy-done, f32[320,3456]{1,0:T(8,128)S(1)} %shard_map.64.wide_ref), custom_call_target="tpu_custom_call" | custom-call | tf_op jit(solution)/shard_map/pallas_call | solution.py:352
  3.0 3.8 %collective-permute-start = (f32[56,320]{1,0:T(8,128)S(1)}, f32[56,320]{1,0:T(8,128)S(1)}, u32[]{:S(2)}, u32[]{:S(2)}) collective-permute-start(f32[56,320]{1,0:T(8,128)S(1)} %shard_map.65.own_ref), channel_id=1, source_target_pairs={{0,2},{1,3},{2,0},{3,1},{4,6},{5,7},{6,4},{7,5},{8,10},{9,11},{10,... | collective-permute-start | bytes 215048 | tf_op jit(solution)/shard_map/ppermute | solution.py:354
  6.8 0.4 collective-permute-start.1
  7.2 2.3 %collective-permute-start.2 = (f32[56,320]{1,0:T(8,128)S(1)}, f32[56,320]{1,0:T(8,128)S(1)}, u32[]{:S(2)}, u32[]{:S(2)}) collective-permute-start(f32[56,320]{1,0:T(8,128)S(1)} %shard_map.65.own_ref), channel_id=1, source_target_pairs={{0,3},{1,0},{2,1},{3,2},{4,7},{5,4},{6,5},{7,6},{8,11},{9,8},{10,9... | collective-permute-start | bytes 215048 | tf_op jit(solution)/shard_map/ppermute | solution.py:354
  9.5 0.1 shard_map.66
  9.7 0.0 collective-permute-done.one_ref
  9.7 3.3 %collective-permute-done.1.two_ref = f32[56,320]{1,0:T(8,128)S(1)} collective-permute-done((f32[56,320]{1,0:T(8,128)S(1)}, f32[56,320]{1,0:T(8,128)S(1)}, u32[]{:S(2)}, u32[]{:S(2)}) %collective-permute-start.1) | collective-permute-done | bytes 71712 | tf_op jit(solution)/shard_map/ppermute | solution.py:354
  13.0 0.8 %shard_map.67 = bf16[32,24,128]{2,1,0:T(8,128)(2,1)S(1)} custom-call(f32[56,320]{1,0:T(8,128)S(1)} %shard_map.65.own_ref, f32[56,320]{1,0:T(8,128)S(1)} %collective-permute-done.one_ref, f32[56,320]{1,0:T(8,128)S(1)} %collective-permute-done.1.two_ref, f32[56,320]{1,0:T(8,128)S(1)} %collective-permute-done.2.three_ref, ...), custom_call_target="tpu_custom_call" | custom-call | tf_op jit(solution)/shard_map/pallas_call | solution.py:360
  13.8 18.7 %all_to_all.5.own_ref = bf16[32,24,128]{2,1,0:T(8,128)(2,1)S(1)} all-to-all(bf16[32,24,128]{2,1,0:T(8,128)(2,1)S(1)} %shard_map.67), channel_id=1, replica_groups={{0,8,16,24,32,40,48,56,64,72,80,88,96,104,112,120,128,136,144,152,160,1..., dimensions={0} | all-to-all | bytes 393216 | tf_op jit(solution)/shard_map/all_to_all | solution.py:368
  32.4 3.8 %collective-permute-start.3 = (bf16[32,24,128]{2,1,0:T(8,128)(2,1)S(1)}, bf16[32,24,128]{2,1,0:T(8,128)(2,1)S(1)}, u32[]{:S(2)}, u32[]{:S(2)}) collective-permute-start(bf16[32,24,128]{2,1,0:T(8,128)(2,1)S(1)} %all_to_all.5.own_ref), channel_id=1, source_target_pairs={{0,4},{4,0},{8,12},{12,8},{16,20},{20,16},{24,28},{28,24},{32,36},... | collective-permute-start | bytes 589832 | tf_op jit(solution)/shard_map/ppermute | solution.py:371
  36.2 2.0 %shard_map.68.sum_ref = f32[2,160,640]{2,1,0:T(8,128)S(1)} custom-call(bf16[32,24,128]{2,1,0:T(8,128)(2,1)S(1)} %all_to_all.5.own_ref), custom_call_target="tpu_custom_call" | custom-call | tf_op jit(solution)/shard_map/pallas_call | solution.py:377
  38.2 2.0 %shard_map.69 = (bf16[2,5,40,128]{3,2,1,0:T(8,128)(2,1)S(1)}, bf16[2,5,40,128]{3,2,1,0:T(8,128)(2,1)S(1)}, bf16[2,5,40,128]{3,2,1,0:T(8,128)(2,1)S(1)}, bf16[2,5,40,128]{3,2,1,0:T(8,128)(2,1)S(1)}) custom-call(bf16[32,24,128]{2,1,0:T(8,128)(2,1)S(1)} %collective-permute-done.3.other_ref, f32[2,160,640]{2,1,0:T(8,128)S(1)} %shard_map.68.sum_ref), custom_call_target="tpu_custom_call" | custom-call | tf_op jit(solution)/shard_map/pallas_call | solution.py:382
  40.2 0.4 collective-permute-start.4
  40.6 1.7 %collective-permute-start.5 = (bf16[2,5,40,128]{3,2,1,0:T(8,128)(2,1)S(1)}, bf16[2,5,40,128]{3,2,1,0:T(8,128)(2,1)S(1)}, u32[]{:S(2)}, u32[]{:S(2)}) collective-permute-start(bf16[2,5,40,128]{3,2,1,0:T(8,128)(2,1)S(1)} %get-tuple-element.15), channel_id=1, source_target_pairs={{0,128},{4,132},{8,136},{12,140},{16,144},{20,148},{24,152},{28,15... | collective-permute-start | bytes 307208 | tf_op jit(solution)/shard_map/ppermute | solution.py:389
  42.3 1.2 %collective-permute-start.6 = (bf16[2,5,40,128]{3,2,1,0:T(8,128)(2,1)S(1)}, bf16[2,5,40,128]{3,2,1,0:T(8,128)(2,1)S(1)}, u32[]{:S(2)}, u32[]{:S(2)}) collective-permute-start(bf16[2,5,40,128]{3,2,1,0:T(8,128)(2,1)S(1)} %get-tuple-element.16), channel_id=1, source_target_pairs={{0,192},{4,196},{8,200},{12,204},{16,208},{20,212},{24,216},{28,22... | collective-permute-start | bytes 307208 | tf_op jit(solution)/shard_map/ppermute | solution.py:389
  43.5 4.7 %collective-permute-done.4.one_ref = bf16[2,5,40,128]{3,2,1,0:T(8,128)(2,1)S(1)} collective-permute-done((bf16[2,5,40,128]{3,2,1,0:T(8,128)(2,1)S(1)}, bf16[2,5,40,128]{3,2,1,0:T(8,128)(2,1)S(1)}, u32[]{:S(2)}, u32[]{:S(2)}) %collective-permute-start.4) | collective-permute-done | bytes 102432 | tf_op jit(solution)/shard_map/ppermute | solution.py:389
  48.2 0.3 collective-permute-done.6.three_ref
  48.4 0.9 %shard_map.70 = bf16[34,40,128]{2,1,0:T(8,128)(2,1)} custom-call(bf16[2,5,40,128]{3,2,1,0:T(8,128)(2,1)S(1)} %get-tuple-element.13.zero_ref, bf16[2,5,40,128]{3,2,1,0:T(8,128)(2,1)S(1)} %collective-permute-done.4.one_ref, bf16[2,5,40,128]{3,2,1,0:T(8,128)(2,1)S(1)} %collective-permute-done.5.two_ref, bf16[2,5,40,128]{3,2,1,0:T(8,128)(2,1)S(1)} %collective-permute-done.6.three_ref), custom_call_target="tpu_custom_call" | custom-call | tf_op jit(solution)/shard_map/pallas_call | solution.py:390
  (11 shorter events, 0.0 us)
Async XLA Ops:
  0.0 1.7 %copy-start = (bf16[320,3456]{1,0:T(8,128)(2,1)S(1)}, bf16[320,3456]{1,0:T(8,128)(2,1)}, u32[]{:S(2)}) copy-start(bf16[320,3456]{1,0:T(8,128)(2,1)} %jac_ref.1) | copy-start | bytes 6635524
  0.0 0.9 %copy-start.2 = (bf16[320,64]{0,1:T(8,128)(2,1)S(1)}, bf16[320,64]{0,1:T(8,128)(2,1)}, u32[]{:S(2)}) copy-start(bf16[320,64]{0,1:T(8,128)(2,1)} %param.7) | copy-start | bytes 122884
  1.7 7.8 %copy-start.5 = (s32[320]{0:T(512)S(1)}, s32[320]{0:T(512)}, u32[]{:S(2)}) copy-start(s32[320]{0:T(512)} %param.10) | copy-start | bytes 3844
  1.7 7.8 %copy-start.1 = (s32[320,54]{0,1:T(8,128)S(1)}, s32[320,54]{0,1:T(8,128)}, u32[]{:S(2)}) copy-start(s32[320,54]{0,1:T(8,128)} %param.8) | copy-start | bytes 207364
  1.8 7.8 %copy-start.3 = (bf16[320,54]{0,1:T(8,128)(2,1)S(1)}, bf16[320,54]{0,1:T(8,128)(2,1)}, u32[]{:S(2)}) copy-start(bf16[320,54]{0,1:T(8,128)(2,1)} %param.9) | copy-start | bytes 103684
  1.8 7.8 %copy-start.4 = (s32[64]{0:T(128)S(1)}, s32[64]{0:T(128)}, u32[]{:S(2)}) copy-start(s32[64]{0:T(128)} %param.11) | copy-start | bytes 772
  3.0 6.7 %collective-permute-start = (f32[56,320]{1,0:T(8,128)S(1)}, f32[56,320]{1,0:T(8,128)S(1)}, u32[]{:S(2)}, u32[]{:S(2)}) collective-permute-start(f32[56,320]{1,0:T(8,128)S(1)} %shard_map.65.own_ref), channel_id=1, source_target_pairs={{0,2},{1,3},{2,0},{3,1},{4,6},{5,7},{6,4},{7,5},{8,10},{9,11},{10,... | collective-permute-start | bytes 215048 | tf_op jit(solution)/shard_map/ppermute | solution.py:354
  6.8 6.1 %collective-permute-start.1 = (f32[56,320]{1,0:T(8,128)S(1)}, f32[56,320]{1,0:T(8,128)S(1)}, u32[]{:S(2)}, u32[]{:S(2)}) collective-permute-start(f32[56,320]{1,0:T(8,128)S(1)} %shard_map.65.own_ref), channel_id=1, source_target_pairs={{0,1},{1,2},{2,3},{3,0},{4,5},{5,6},{6,7},{7,4},{8,9},{9,10},{10,1... | collective-permute-start | bytes 215048 | tf_op jit(solution)/shard_map/ppermute | solution.py:354
  7.2 5.7 %collective-permute-start.2 = (f32[56,320]{1,0:T(8,128)S(1)}, f32[56,320]{1,0:T(8,128)S(1)}, u32[]{:S(2)}, u32[]{:S(2)}) collective-permute-start(f32[56,320]{1,0:T(8,128)S(1)} %shard_map.65.own_ref), channel_id=1, source_target_pairs={{0,3},{1,0},{2,1},{3,2},{4,7},{5,4},{6,5},{7,6},{8,11},{9,8},{10,9... | collective-permute-start | bytes 215048 | tf_op jit(solution)/shard_map/ppermute | solution.py:354
  32.4 5.8 %collective-permute-start.3 = (bf16[32,24,128]{2,1,0:T(8,128)(2,1)S(1)}, bf16[32,24,128]{2,1,0:T(8,128)(2,1)S(1)}, u32[]{:S(2)}, u32[]{:S(2)}) collective-permute-start(bf16[32,24,128]{2,1,0:T(8,128)(2,1)S(1)} %all_to_all.5.own_ref), channel_id=1, source_target_pairs={{0,4},{4,0},{8,12},{12,8},{16,20},{20,16},{24,28},{28,24},{32,36},... | collective-permute-start | bytes 589832 | tf_op jit(solution)/shard_map/ppermute | solution.py:371
  40.2 8.0 %collective-permute-start.4 = (bf16[2,5,40,128]{3,2,1,0:T(8,128)(2,1)S(1)}, bf16[2,5,40,128]{3,2,1,0:T(8,128)(2,1)S(1)}, u32[]{:S(2)}, u32[]{:S(2)}) collective-permute-start(bf16[2,5,40,128]{3,2,1,0:T(8,128)(2,1)S(1)} %get-tuple-element.14), channel_id=1, source_target_pairs={{0,64},{4,68},{8,72},{12,76},{16,80},{20,84},{24,88},{28,92},{32,9... | collective-permute-start | bytes 307208 | tf_op jit(solution)/shard_map/ppermute | solution.py:389
  40.6 7.6 %collective-permute-start.5 = (bf16[2,5,40,128]{3,2,1,0:T(8,128)(2,1)S(1)}, bf16[2,5,40,128]{3,2,1,0:T(8,128)(2,1)S(1)}, u32[]{:S(2)}, u32[]{:S(2)}) collective-permute-start(bf16[2,5,40,128]{3,2,1,0:T(8,128)(2,1)S(1)} %get-tuple-element.15), channel_id=1, source_target_pairs={{0,128},{4,132},{8,136},{12,140},{16,144},{20,148},{24,152},{28,15... | collective-permute-start | bytes 307208 | tf_op jit(solution)/shard_map/ppermute | solution.py:389
  42.3 6.1 %collective-permute-start.6 = (bf16[2,5,40,128]{3,2,1,0:T(8,128)(2,1)S(1)}, bf16[2,5,40,128]{3,2,1,0:T(8,128)(2,1)S(1)}, u32[]{:S(2)}, u32[]{:S(2)}) collective-permute-start(bf16[2,5,40,128]{3,2,1,0:T(8,128)(2,1)S(1)} %get-tuple-element.16), channel_id=1, source_target_pairs={{0,192},{4,196},{8,200},{12,204},{16,208},{20,212},{24,216},{28,22... | collective-permute-start | bytes 307208 | tf_op jit(solution)/shard_map/ppermute | solution.py:389

commit v5 on v4

--- a/solution.py
+++ b/solution.py
@@ -11,6 +11,8 @@
 KL = 54
 KP = 56
 SHARE = 34
+ROOM = 40
+PACKED = 144
 NLON = 2688
 ROWS = 2
 CAP = 5
@@ -95,11 +97,19 @@
         product = product[:, :half] + product[:, half:]
         high = product.astype(BF16)
         low = (product - high.astype(F32)).astype(BF16)
-        out_ref[:, records] = dot_nt(select, high) + dot_nt(select, low)
-
-
-def prepare_kernel(index_ref, weight_ref, column_ref, count_ref, place_ref, aux_ref):
-    place_ref[...] = index_ref[...].astype(F32) + weight_ref[...].astype(F32)
+        total = dot_nt(select, high) + dot_nt(select, low)
+        if size == LANES:
+            out_ref[KP * start // LANES : KP * start // LANES + KP, :] = total
+        else:
+            wide_total = jnp.concatenate([total, jnp.zeros_like(total)], axis=1)
+            upper = pltpu.roll(wide_total[32:], size, 1)
+            out_ref[2 * KP :, :] = wide_total[:32] + jnp.concatenate(
+                [upper, jnp.zeros((8, LANES), F32)], axis=0
+            )
+
+
+def prepare_kernel(index_ref, weight_ref, column_ref, count_ref, hat_ref, aux_ref):
+    place = index_ref[...].astype(F32) + weight_ref[...].astype(F32)
     lanes = lane_iota((8, RECS))
     band = floor_div(lanes, CAP)
     slot = lanes.astype(F32) - CAP * band
@@ -115,23 +125,23 @@
     high = lax.shift_right_logical(column, 5)
     low = column - high * LOW
     which = row_iota((8, RECS))
-    aux_ref[...] = jnp.where(
-        which == 0, live, jnp.where(which == 2, high.astype(F32), low.astype(F32))
-    )
-
-
-def pack_kernel(own_ref, one_ref, two_ref, three_ref, place_ref, aux_ref, out_ref, sum_ref):
-    sum_ref[...] = (own_ref[...] + one_ref[...]) + (two_ref[...] + three_ref[...])
+    aux_ref[...] = jnp.where(which == 2, high.astype(F32), low.astype(F32))
     first = lax.axis_index("lev") * SHARE
-    live = aux_ref[0:1, :]
-    blocks = []
-    for start, size in ((0, 24), (24, 8), (32, 8)):
-        target = (row_iota((size, RECS)) + (first + start)).astype(F32)
-        total = jnp.zeros((size, RECS), F32)
-        for k in range(KL):
-            hat = jnp.maximum(1.0 - jnp.abs(target - place_ref[k : k + 1, :]), 0.0)
-            total = total + hat * sum_ref[k : k + 1, :]
-        blocks.append(total * live)
+    target = (row_iota((ROOM, RECS)) + first).astype(F32)
+    for k in range(KL):
+        hat_ref[k] = jnp.maximum(1.0 - jnp.abs(target - place[k : k + 1, :]), 0.0) * live[0:1, :]
+
+
+def pack_kernel(own_ref, one_ref, two_ref, three_ref, hat_ref, aux_ref, out_ref, sum_ref):
+    total = (own_ref[...] + one_ref[...]) + (two_ref[...] + three_ref[...])
+    sum_ref[:, 0:LANES] = total[0:KP]
+    sum_ref[:, LANES : 2 * LANES] = total[KP : 2 * KP]
+    sum_ref[0:32, 2 * LANES :] = total[2 * KP :]
+    sum_ref[32:, 2 * LANES :] = pltpu.roll(total[2 * KP : 2 * KP + 24], 64, 1)
+    profile = jnp.zeros((ROOM, RECS), F32)
+    for k in range(KL):
+        profile = profile + hat_ref[k] * sum_ref[k : k + 1, 0:RECS]
+    blocks = [profile[0:24], profile[24:32], profile[32:40]]
     which = row_iota((8, RECS))
     blocks[2] = jnp.where(which < 2, blocks[2], jnp.where(which < 4, aux_ref[...], 0.0))
     full = 3 * LANES
@@ -349,19 +359,19 @@
     vmem = pl.BlockSpec(memory_space=pltpu.VMEM)
     hbm = pl.BlockSpec(memory_space=pltpu.HBM)
     wide = call(spread_kernel, jax.ShapeDtypeStruct((RECS, WIDTH), F32))(departures.T)
-    partial = call(contract_kernel, jax.ShapeDtypeStruct((KP, RECS), F32))(jacobian, wide)
+    partial = call(contract_kernel, jax.ShapeDtypeStruct((PACKED, LANES), F32))(jacobian, wide)
     others = [
         lax.ppermute(partial, "lev", [(i, (i + k) % 4) for i in range(4)]) for k in (2, 1, 3)
     ]
-    place, aux = call(
+    hat, aux = call(
         prepare_kernel,
-        (jax.ShapeDtypeStruct((KL, RECS), F32), jax.ShapeDtypeStruct((8, RECS), F32)),
+        (jax.ShapeDtypeStruct((KL, ROOM, RECS), F32), jax.ShapeDtypeStruct((8, RECS), F32)),
     )(level_index.T, level_weight.T, column_index.reshape(1, RECS), record_counts.reshape(1, BANDS))
     packed = call(
         pack_kernel,
         jax.ShapeDtypeStruct((SENDERS, 24, LANES), BF16),
-        [pltpu.VMEM((KP, RECS), F32)],
-    )(partial, *others, place, aux)
+        [pltpu.VMEM((KP, 3 * LANES), F32)],
+    )(partial, *others, hat, aux)
     same_core = [
         [x * 16 + z * 2 + c for x in range(XS) for z in range(ZS)] for c in range(CORES)
     ]

time: 49.4 us -> 49 us (level)
  waiting for transfers between devices: 8.22 us -> 7.16 us
    ppermute x3, waiting for transfers between devices: 3.29 us -> 2.23 us  [local(): lax.ppermute(partial, 'lev', [(i, (i + k) % 4) for i in range(4)])]
    pallas_call x2, Pallas kernels: 1.37 us -> 1.97 us  [the longest x1 1.31 us: local(): call(contract_kernel, jax.ShapeDtypeStruct((PACKED, LANES), F32))]
  transfers between devices with their start and end apart: 7 -> 7, of which waited for: 3 -> 3; matrix products, arithmetic and copies ran while one was open for 0% -> 0% of each run, Pallas kernels for 4% -> 5%
where the time goes in v5:
time: 49 us; the launch traced here: 48.8 us
  blocking collectives  19 us (39%)
  starting transfers between devices  13.6 us (28%)
  Pallas kernels  7.98 us (16%)
  waiting for transfers between devices  7.16 us (15%)
  local copies, waits for them, and re-layouts  0.98 us (2%)
    all_to_all x1, blocking collectives, local(): lax.all_to_all(packed, 'band', split_axis=0, concat_axis=0, axis_index_gr...  19 us
    ppermute x3, starting transfers between devices, local(): lax.ppermute(partial, 'lev', [(i, (i + k) % 4) for i in range(4)])  6.45 us
    ppermute x3, waiting for transfers between devices, local(): received[k] = lax.ppermute(spectra[k], 'band', x_shift(k))  4.92 us
    ppermute x1, starting transfers between devices, local(): other = lax.ppermute(arrived, 'band', [(i, i ^ 1) for i in range(BANDS)])  3.79 us
    ppermute x3, starting transfers between devices, local(): received[k] = lax.ppermute(spectra[k], 'band', x_shift(k))  3.32 us
    ppermute x3, waiting for transfers between devices, local(): lax.ppermute(partial, 'lev', [(i, (i + k) % 4) for i in range(4)])  2.23 us
    pallas_call x1, Pallas kernels, local(): call(transform_other_kernel, [jax.ShapeDtypeStruct((CORES, PARTS, COEFS,...  1.98 us
    pallas_call x1, Pallas kernels, local(): call(transform_own_kernel, jax.ShapeDtypeStruct((CORES, XS * COEFS, PARTS...  1.96 us
  transfers between devices with their start and end apart: 7, of which 3 were waited for; matrix products, arithmetic and copies ran while one was open for 0% of the time, Pallas kernels for 5%

profile of v5, /device:TPU:1, one launch (start us, length us, event | category | flops | bytes accessed | tf_op | source)
XLA Modules:
  0.0 48.8 jit_solution(10009892742427270156)
XLA Ops:
  0.0 0.9 %copy-done.2 = bf16[320,64]{0,1:T(8,128)(2,1)S(1)} copy-done((bf16[320,64]{0,1:T(8,128)(2,1)S(1)}, bf16[320,64]{0,1:T(8,128)(2,1)}, u32[]{:S(2)}) %copy-start.2) | copy-done | bytes 40984
  1.0 0.8 %shard_map.64.wide_ref = f32[320,3456]{1,0:T(8,128)S(1)} custom-call(bf16[64,320]{1,0:T(8,128)(2,1)S(1)} %bitcast.6), custom_call_target="tpu_custom_call" | custom-call | tf_op jit(solution)/shard_map/pallas_call | solution.py:361
  1.7 0.0 copy-start.5
  1.7 0.0 copy-start.1
  1.8 0.0 copy-start.3
  1.8 0.0 copy-start.4
  1.8 1.3 %shard_map.65.own_ref = f32[144,128]{1,0:T(8,128)S(1)} custom-call(bf16[320,3456]{1,0:T(8,128)(2,1)S(1)} %copy-done, f32[320,3456]{1,0:T(8,128)S(1)} %shard_map.64.wide_ref), custom_call_target="tpu_custom_call" | custom-call | tf_op jit(solution)/shard_map/pallas_call | solution.py:362
  3.1 3.8 %collective-permute-start = (f32[144,128]{1,0:T(8,128)S(1)}, f32[144,128]{1,0:T(8,128)S(1)}, u32[]{:S(2)}, u32[]{:S(2)}) collective-permute-start(f32[144,128]{1,0:T(8,128)S(1)} %shard_map.65.own_ref), channel_id=1, source_target_pairs={{0,2},{1,3},{2,0},{3,1},{4,6},{5,7},{6,4},{7,5},{8,10},{9,11},{10,... | collective-permute-start | bytes 221192 | tf_op jit(solution)/shard_map/ppermute | solution.py:364
  6.9 0.4 collective-permute-start.1
  7.3 2.3 %collective-permute-start.2 = (f32[144,128]{1,0:T(8,128)S(1)}, f32[144,128]{1,0:T(8,128)S(1)}, u32[]{:S(2)}, u32[]{:S(2)}) collective-permute-start(f32[144,128]{1,0:T(8,128)S(1)} %shard_map.65.own_ref), channel_id=1, source_target_pairs={{0,3},{1,0},{2,1},{3,2},{4,7},{5,4},{6,5},{7,6},{8,11},{9,8},{10,9... | collective-permute-start | bytes 221192 | tf_op jit(solution)/shard_map/ppermute | solution.py:364
  9.6 0.7 %shard_map.66 = (f32[54,40,320]{2,1,0:T(8,128)S(1)}, f32[8,320]{1,0:T(8,128)S(1)}) custom-call(s32[54,320]{1,0:T(8,128)S(1)} %bitcast.5, bf16[54,320]{1,0:T(8,128)(2,1)S(1)} %bitcast.7, s32[1,320]{1,0:T(1,128)S(1)} %reshape.6.column_ref, s32[1,64]{1,0:T(1,128)S(1)} %bitcast.8), custom_call_target="tpu_custom_call" | custom-call | tf_op jit(solution)/shard_map/pallas_call | solution.py:366
  10.2 2.2 %collective-permute-done.1.two_ref = f32[144,128]{1,0:T(8,128)S(1)} collective-permute-done((f32[144,128]{1,0:T(8,128)S(1)}, f32[144,128]{1,0:T(8,128)S(1)}, u32[]{:S(2)}, u32[]{:S(2)}) %collective-permute-start.1) | collective-permute-done | bytes 73760 | tf_op jit(solution)/shard_map/ppermute | solution.py:364
  12.5 0.0 collective-permute-done.2.three_ref
  12.5 0.4 shard_map.67
  12.9 19.0 %all_to_all.5.own_ref = bf16[32,24,128]{2,1,0:T(8,128)(2,1)S(1)} all-to-all(bf16[32,24,128]{2,1,0:T(8,128)(2,1)S(1)} %shard_map.67), channel_id=1, replica_groups={{0,8,16,24,32,40,48,56,64,72,80,88,96,104,112,120,128,136,144,152,160,1..., dimensions={0} | all-to-all | bytes 393216 | tf_op jit(solution)/shard_map/all_to_all | solution.py:378
  31.9 3.8 %collective-permute-start.3 = (bf16[32,24,128]{2,1,0:T(8,128)(2,1)S(1)}, bf16[32,24,128]{2,1,0:T(8,128)(2,1)S(1)}, u32[]{:S(2)}, u32[]{:S(2)}) collective-permute-start(bf16[32,24,128]{2,1,0:T(8,128)(2,1)S(1)} %all_to_all.5.own_ref), channel_id=1, source_target_pairs={{0,4},{4,0},{8,12},{12,8},{16,20},{20,16},{24,28},{28,24},{32,36},... | collective-permute-start | bytes 589832 | tf_op jit(solution)/shard_map/ppermute | solution.py:381
  35.7 2.0 %shard_map.68.sum_ref = f32[2,160,640]{2,1,0:T(8,128)S(1)} custom-call(bf16[32,24,128]{2,1,0:T(8,128)(2,1)S(1)} %all_to_all.5.own_ref), custom_call_target="tpu_custom_call" | custom-call | tf_op jit(solution)/shard_map/pallas_call | solution.py:387
  37.7 2.0 %shard_map.69 = (bf16[2,5,40,128]{3,2,1,0:T(8,128)(2,1)S(1)}, bf16[2,5,40,128]{3,2,1,0:T(8,128)(2,1)S(1)}, bf16[2,5,40,128]{3,2,1,0:T(8,128)(2,1)S(1)}, bf16[2,5,40,128]{3,2,1,0:T(8,128)(2,1)S(1)}) custom-call(bf16[32,24,128]{2,1,0:T(8,128)(2,1)S(1)} %collective-permute-done.3.other_ref, f32[2,160,640]{2,1,0:T(8,128)S(1)} %shard_map.68.sum_ref), custom_call_target="tpu_custom_call" | custom-call | tf_op jit(solution)/shard_map/pallas_call | solution.py:392
  39.7 0.4 collective-permute-start.4
  40.1 1.7 %collective-permute-start.5 = (bf16[2,5,40,128]{3,2,1,0:T(8,128)(2,1)S(1)}, bf16[2,5,40,128]{3,2,1,0:T(8,128)(2,1)S(1)}, u32[]{:S(2)}, u32[]{:S(2)}) collective-permute-start(bf16[2,5,40,128]{3,2,1,0:T(8,128)(2,1)S(1)} %get-tuple-element.15), channel_id=1, source_target_pairs={{0,128},{4,132},{8,136},{12,140},{16,144},{20,148},{24,152},{28,15... | collective-permute-start | bytes 307208 | tf_op jit(solution)/shard_map/ppermute | solution.py:399
  41.8 1.2 %collective-permute-start.6 = (bf16[2,5,40,128]{3,2,1,0:T(8,128)(2,1)S(1)}, bf16[2,5,40,128]{3,2,1,0:T(8,128)(2,1)S(1)}, u32[]{:S(2)}, u32[]{:S(2)}) collective-permute-start(bf16[2,5,40,128]{3,2,1,0:T(8,128)(2,1)S(1)} %get-tuple-element.16), channel_id=1, source_target_pairs={{0,192},{4,196},{8,200},{12,204},{16,208},{20,212},{24,216},{28,22... | collective-permute-start | bytes 307208 | tf_op jit(solution)/shard_map/ppermute | solution.py:399
  43.0 4.7 %collective-permute-done.4.one_ref = bf16[2,5,40,128]{3,2,1,0:T(8,128)(2,1)S(1)} collective-permute-done((bf16[2,5,40,128]{3,2,1,0:T(8,128)(2,1)S(1)}, bf16[2,5,40,128]{3,2,1,0:T(8,128)(2,1)S(1)}, u32[]{:S(2)}, u32[]{:S(2)}) %collective-permute-start.4) | collective-permute-done | bytes 102432 | tf_op jit(solution)/shard_map/ppermute | solution.py:399
  47.7 0.3 collective-permute-done.6.three_ref
  47.9 0.9 %shard_map.70 = bf16[34,40,128]{2,1,0:T(8,128)(2,1)} custom-call(bf16[2,5,40,128]{3,2,1,0:T(8,128)(2,1)S(1)} %get-tuple-element.13.zero_ref, bf16[2,5,40,128]{3,2,1,0:T(8,128)(2,1)S(1)} %collective-permute-done.4.one_ref, bf16[2,5,40,128]{3,2,1,0:T(8,128)(2,1)S(1)} %collective-permute-done.5.two_ref, bf16[2,5,40,128]{3,2,1,0:T(8,128)(2,1)S(1)} %collective-permute-done.6.three_ref), custom_call_target="tpu_custom_call" | custom-call | tf_op jit(solution)/shard_map/pallas_call | solution.py:400
  (11 shorter events, 0.0 us)
Async XLA Ops:
  0.0 1.7 %copy-start = (bf16[320,3456]{1,0:T(8,128)(2,1)S(1)}, bf16[320,3456]{1,0:T(8,128)(2,1)}, u32[]{:S(2)}) copy-start(bf16[320,3456]{1,0:T(8,128)(2,1)} %jac_ref.1) | copy-start | bytes 6635524
  0.0 0.9 %copy-start.2 = (bf16[320,64]{0,1:T(8,128)(2,1)S(1)}, bf16[320,64]{0,1:T(8,128)(2,1)}, u32[]{:S(2)}) copy-start(bf16[320,64]{0,1:T(8,128)(2,1)} %param.7) | copy-start | bytes 122884
  1.7 7.8 %copy-start.5 = (s32[320]{0:T(512)S(1)}, s32[320]{0:T(512)}, u32[]{:S(2)}) copy-start(s32[320]{0:T(512)} %param.10) | copy-start | bytes 3844
  1.7 7.8 %copy-start.1 = (s32[320,54]{0,1:T(8,128)S(1)}, s32[320,54]{0,1:T(8,128)}, u32[]{:S(2)}) copy-start(s32[320,54]{0,1:T(8,128)} %param.8) | copy-start | bytes 207364
  1.8 7.8 %copy-start.3 = (bf16[320,54]{0,1:T(8,128)(2,1)S(1)}, bf16[320,54]{0,1:T(8,128)(2,1)}, u32[]{:S(2)}) copy-start(bf16[320,54]{0,1:T(8,128)(2,1)} %param.9) | copy-start | bytes 103684
  1.8 7.8 %copy-start.4 = (s32[64]{0:T(128)S(1)}, s32[64]{0:T(128)}, u32[]{:S(2)}) copy-start(s32[64]{0:T(128)} %param.11) | copy-start | bytes 772
  3.1 7.1 %collective-permute-start = (f32[144,128]{1,0:T(8,128)S(1)}, f32[144,128]{1,0:T(8,128)S(1)}, u32[]{:S(2)}, u32[]{:S(2)}) collective-permute-start(f32[144,128]{1,0:T(8,128)S(1)} %shard_map.65.own_ref), channel_id=1, source_target_pairs={{0,2},{1,3},{2,0},{3,1},{4,6},{5,7},{6,4},{7,5},{8,10},{9,11},{10,... | collective-permute-start | bytes 221192 | tf_op jit(solution)/shard_map/ppermute | solution.py:364
  6.9 5.6 %collective-permute-start.1 = (f32[144,128]{1,0:T(8,128)S(1)}, f32[144,128]{1,0:T(8,128)S(1)}, u32[]{:S(2)}, u32[]{:S(2)}) collective-permute-start(f32[144,128]{1,0:T(8,128)S(1)} %shard_map.65.own_ref), channel_id=1, source_target_pairs={{0,1},{1,2},{2,3},{3,0},{4,5},{5,6},{6,7},{7,4},{8,9},{9,10},{10,1... | collective-permute-start | bytes 221192 | tf_op jit(solution)/shard_map/ppermute | solution.py:364
  7.3 5.2 %collective-permute-start.2 = (f32[144,128]{1,0:T(8,128)S(1)}, f32[144,128]{1,0:T(8,128)S(1)}, u32[]{:S(2)}, u32[]{:S(2)}) collective-permute-start(f32[144,128]{1,0:T(8,128)S(1)} %shard_map.65.own_ref), channel_id=1, source_target_pairs={{0,3},{1,0},{2,1},{3,2},{4,7},{5,4},{6,5},{7,6},{8,11},{9,8},{10,9... | collective-permute-start | bytes 221192 | tf_op jit(solution)/shard_map/ppermute | solution.py:364
  31.9 5.8 %collective-permute-start.3 = (bf16[32,24,128]{2,1,0:T(8,128)(2,1)S(1)}, bf16[32,24,128]{2,1,0:T(8,128)(2,1)S(1)}, u32[]{:S(2)}, u32[]{:S(2)}) collective-permute-start(bf16[32,24,128]{2,1,0:T(8,128)(2,1)S(1)} %all_to_all.5.own_ref), channel_id=1, source_target_pairs={{0,4},{4,0},{8,12},{12,8},{16,20},{20,16},{24,28},{28,24},{32,36},... | collective-permute-start | bytes 589832 | tf_op jit(solution)/shard_map/ppermute | solution.py:381
  39.7 8.0 %collective-permute-start.4 = (bf16[2,5,40,128]{3,2,1,0:T(8,128)(2,1)S(1)}, bf16[2,5,40,128]{3,2,1,0:T(8,128)(2,1)S(1)}, u32[]{:S(2)}, u32[]{:S(2)}) collective-permute-start(bf16[2,5,40,128]{3,2,1,0:T(8,128)(2,1)S(1)} %get-tuple-element.14), channel_id=1, source_target_pairs={{0,64},{4,68},{8,72},{12,76},{16,80},{20,84},{24,88},{28,92},{32,9... | collective-permute-start | bytes 307208 | tf_op jit(solution)/shard_map/ppermute | solution.py:399
  40.1 7.6 %collective-permute-start.5 = (bf16[2,5,40,128]{3,2,1,0:T(8,128)(2,1)S(1)}, bf16[2,5,40,128]{3,2,1,0:T(8,128)(2,1)S(1)}, u32[]{:S(2)}, u32[]{:S(2)}) collective-permute-start(bf16[2,5,40,128]{3,2,1,0:T(8,128)(2,1)S(1)} %get-tuple-element.15), channel_id=1, source_target_pairs={{0,128},{4,132},{8,136},{12,140},{16,144},{20,148},{24,152},{28,15... | collective-permute-start | bytes 307208 | tf_op jit(solution)/shard_map/ppermute | solution.py:399
  41.8 6.1 %collective-permute-start.6 = (bf16[2,5,40,128]{3,2,1,0:T(8,128)(2,1)S(1)}, bf16[2,5,40,128]{3,2,1,0:T(8,128)(2,1)S(1)}, u32[]{:S(2)}, u32[]{:S(2)}) collective-permute-start(bf16[2,5,40,128]{3,2,1,0:T(8,128)(2,1)S(1)} %get-tuple-element.16), channel_id=1, source_target_pairs={{0,192},{4,196},{8,200},{12,204},{16,208},{20,212},{24,216},{28,22... | collective-permute-start | bytes 307208 | tf_op jit(solution)/shard_map/ppermute | solution.py:399

commit v6 on v5

--- a/solution.py
+++ b/solution.py
@@ -209,7 +209,6 @@
     step_rows = row_iota((16, LANES)).astype(F32)
     which = row_iota((16, LANES))
     even = jnp.bitwise_and(row_iota((8, LANES)), 1) == 0
-    left_ref[SHARE * 16 :, :] = jnp.zeros((PARTS * LANES - SHARE * 16, DEPTH), BF16)
 
     for v in range(TILES):
         columns = slice(LANES * v, LANES * (v + 1))
@@ -272,7 +271,7 @@
             between[v // 3]()
 
 
-SPANS = ((0, 256), (256, 256), (512, 128))
+SPANS = ((0, 256), (256, 256), (512, 32))
 
 
 def transform_own_kernel(own_ref, sum_ref, *scratch):
@@ -293,6 +292,13 @@
 def transform_other_kernel(other_ref, sum_ref, out0_ref, out1_ref, out2_ref, out3_ref, *scratch):
     outs = (out0_ref, out1_ref, out2_ref, out3_ref)
     blocks, lefts, tables = scratch[0:2], scratch[2:4], scratch[4:6]
+
+    short = {}
+
+    def turned(result, c, k):
+        group = (2 * (-k % XS) + c) % GROUPS
+        piece = result[COEFS * k : COEFS * (k + 1)]
+        return pltpu.roll(piece, 16 * group, 1) if group else piece
 
     def multiply(c, start, size):
         result = sum_ref[c, :, start : start + size] + dot_nt(
@@ -300,11 +306,18 @@
         )
         for part in range(size // LANES):
             for k in range(XS):
-                group = (2 * (-k % XS) + c) % GROUPS
-                piece = result[COEFS * k : COEFS * (k + 1), LANES * part : LANES * (part + 1)]
-                if group:
-                    piece = pltpu.roll(piece, 16 * group, 1)
-                outs[k][c, start // LANES + part] = piece.astype(BF16)
+                outs[k][4 * c + start // LANES + part] = turned(
+                    result[:, LANES * part : LANES * (part + 1)], c, k
+                ).astype(BF16)
+        if size < LANES:
+            short[c] = jnp.concatenate(
+                [result, jnp.zeros((XS * COEFS, LANES - size), F32)], axis=1
+            )
+            if len(short) == CORES:
+                for k in range(XS):
+                    outs[k][8] = (
+                        turned(short[0], 0, k) + pltpu.roll(turned(short[1], 1, k), 64, 1)
+                    ).astype(BF16)
 
     transform(other_ref, 0, blocks[0], lefts[0], tables[0])
     steps = [functools.partial(multiply, 0, *span) for span in SPANS]
@@ -319,7 +332,12 @@
     sources = (zero_ref, three_ref, two_ref, one_ref)
     copies = []
     for part in range(PARTS):
-        values = [sources[g // 2][g % 2, part].astype(F32) for g in range(GROUPS)]
+        values = [
+            sources[g // 2][4 * (g % 2) + part if part < 4 else 8].astype(F32)
+            for g in range(GROUPS)
+        ]
+        if part == 4:
+            values = [pltpu.roll(v, 64, 1) if g % 2 else v for g, v in enumerate(values)]
         first = part * TOGETHER
         count = min(TOGETHER, SHARE - first)
         for bit in (4, 2, 1):
@@ -381,7 +399,7 @@
     other = lax.ppermute(arrived, "band", [(i, i ^ 1) for i in range(BANDS)])
     scratch = (
         [pltpu.VMEM((TILES, 5, 8, LANES), F32)] * CORES
-        + [pltpu.VMEM((PARTS * LANES, DEPTH), BF16)] * CORES
+        + [pltpu.VMEM((SHARE * 16, DEPTH), BF16)] * CORES
         + [pltpu.VMEM((XS * COEFS, DEPTH), BF16)] * CORES
     )
     own_sum = call(
@@ -391,7 +409,7 @@
     )(arrived)
     spectra = call(
         transform_other_kernel,
-        [jax.ShapeDtypeStruct((CORES, PARTS, COEFS, LANES), BF16)] * XS,
+        [jax.ShapeDtypeStruct((9, COEFS, LANES), BF16)] * XS,
         scratch,
     )(other, own_sum)
     received = [spectra[0]] + [None] * 3

time: 49 us -> 48.6 us (level)
  no operation moved by 1% of the time
where the time goes in v6:
time: 48.6 us; the launch traced here: 48.5 us
  blocking collectives  19 us (39%)
  starting transfers between devices  13.6 us (28%)
  Pallas kernels  8.06 us (17%)
  waiting for transfers between devices  6.72 us (14%)
  local copies, waits for them, and re-layouts  0.98 us (2%)
    all_to_all x1, blocking collectives, local(): lax.all_to_all(packed, 'band', split_axis=0, concat_axis=0, axis_index_gr...  19 us
    ppermute x3, starting transfers between devices, local(): lax.ppermute(partial, 'lev', [(i, (i + k) % 4) for i in range(4)])  6.45 us
    ppermute x3, waiting for transfers between devices, local(): received[k] = lax.ppermute(spectra[k], 'band', x_shift(k))  4.48 us
    ppermute x1, starting transfers between devices, local(): other = lax.ppermute(arrived, 'band', [(i, i ^ 1) for i in range(BANDS)])  3.79 us
    ppermute x3, starting transfers between devices, local(): received[k] = lax.ppermute(spectra[k], 'band', x_shift(k))  3.33 us
    ppermute x3, waiting for transfers between devices, local(): lax.ppermute(partial, 'lev', [(i, (i + k) % 4) for i in range(4)])  2.23 us
    pallas_call x1, Pallas kernels, local(): call(transform_other_kernel, [jax.ShapeDtypeStruct((9, COEFS, LANES), BF1...  2.1 us
    pallas_call x1, Pallas kernels, local(): call(transform_own_kernel, jax.ShapeDtypeStruct((CORES, XS * COEFS, PARTS...  1.92 us
  transfers between devices with their start and end apart: 7, of which 3 were waited for; matrix products, arithmetic and copies ran while one was open for 0% of the time, Pallas kernels for 5%

profile of v6, /device:TPU:1, one launch (start us, length us, event | category | flops | bytes accessed | tf_op | source)
XLA Modules:
  0.0 48.5 jit_solution(3130012436235863639)
XLA Ops:
  0.0 0.9 %copy-done.2 = bf16[320,64]{0,1:T(8,128)(2,1)S(1)} copy-done((bf16[320,64]{0,1:T(8,128)(2,1)S(1)}, bf16[320,64]{0,1:T(8,128)(2,1)}, u32[]{:S(2)}) %copy-start.2) | copy-done | bytes 40984
  1.0 0.8 %shard_map.64.wide_ref = f32[320,3456]{1,0:T(8,128)S(1)} custom-call(bf16[64,320]{1,0:T(8,128)(2,1)S(1)} %bitcast.6), custom_call_target="tpu_custom_call" | custom-call | tf_op jit(solution)/shard_map/pallas_call | solution.py:379
  1.7 0.0 copy-start.5
  1.7 0.0 copy-start.1
  1.8 0.0 copy-start.3
  1.8 0.0 copy-start.4
  1.8 1.3 %shard_map.65.own_ref = f32[144,128]{1,0:T(8,128)S(1)} custom-call(bf16[320,3456]{1,0:T(8,128)(2,1)S(1)} %copy-done, f32[320,3456]{1,0:T(8,128)S(1)} %shard_map.64.wide_ref), custom_call_target="tpu_custom_call" | custom-call | tf_op jit(solution)/shard_map/pallas_call | solution.py:380
  3.1 3.8 %collective-permute-start = (f32[144,128]{1,0:T(8,128)S(1)}, f32[144,128]{1,0:T(8,128)S(1)}, u32[]{:S(2)}, u32[]{:S(2)}) collective-permute-start(f32[144,128]{1,0:T(8,128)S(1)} %shard_map.65.own_ref), channel_id=1, source_target_pairs={{0,2},{1,3},{2,0},{3,1},{4,6},{5,7},{6,4},{7,5},{8,10},{9,11},{10,... | collective-permute-start | bytes 221192 | tf_op jit(solution)/shard_map/ppermute | solution.py:382
  6.9 0.4 collective-permute-start.1
  7.3 2.3 %collective-permute-start.2 = (f32[144,128]{1,0:T(8,128)S(1)}, f32[144,128]{1,0:T(8,128)S(1)}, u32[]{:S(2)}, u32[]{:S(2)}) collective-permute-start(f32[144,128]{1,0:T(8,128)S(1)} %shard_map.65.own_ref), channel_id=1, source_target_pairs={{0,3},{1,0},{2,1},{3,2},{4,7},{5,4},{6,5},{7,6},{8,11},{9,8},{10,9... | collective-permute-start | bytes 221192 | tf_op jit(solution)/shard_map/ppermute | solution.py:382
  9.6 0.7 %shard_map.66 = (f32[54,40,320]{2,1,0:T(8,128)S(1)}, f32[8,320]{1,0:T(8,128)S(1)}) custom-call(s32[54,320]{1,0:T(8,128)S(1)} %bitcast.5, bf16[54,320]{1,0:T(8,128)(2,1)S(1)} %bitcast.7, s32[1,320]{1,0:T(1,128)S(1)} %reshape.6.column_ref, s32[1,64]{1,0:T(1,128)S(1)} %bitcast.8), custom_call_target="tpu_custom_call" | custom-call | tf_op jit(solution)/shard_map/pallas_call | solution.py:384
  10.2 0.0 collective-permute-done.one_ref
  10.2 2.2 %collective-permute-done.1.two_ref = f32[144,128]{1,0:T(8,128)S(1)} collective-permute-done((f32[144,128]{1,0:T(8,128)S(1)}, f32[144,128]{1,0:T(8,128)S(1)}, u32[]{:S(2)}, u32[]{:S(2)}) %collective-permute-start.1) | collective-permute-done | bytes 73760 | tf_op jit(solution)/shard_map/ppermute | solution.py:382
  12.5 0.4 shard_map.67
  12.9 19.0 %all_to_all.5.own_ref = bf16[32,24,128]{2,1,0:T(8,128)(2,1)S(1)} all-to-all(bf16[32,24,128]{2,1,0:T(8,128)(2,1)S(1)} %shard_map.67), channel_id=1, replica_groups={{0,8,16,24,32,40,48,56,64,72,80,88,96,104,112,120,128,136,144,152,160,1..., dimensions={0} | all-to-all | bytes 393216 | tf_op jit(solution)/shard_map/all_to_all | solution.py:396
  31.9 3.8 %collective-permute-start.3 = (bf16[32,24,128]{2,1,0:T(8,128)(2,1)S(1)}, bf16[32,24,128]{2,1,0:T(8,128)(2,1)S(1)}, u32[]{:S(2)}, u32[]{:S(2)}) collective-permute-start(bf16[32,24,128]{2,1,0:T(8,128)(2,1)S(1)} %all_to_all.5.own_ref), channel_id=1, source_target_pairs={{0,4},{4,0},{8,12},{12,8},{16,20},{20,16},{24,28},{28,24},{32,36},... | collective-permute-start | bytes 589832 | tf_op jit(solution)/shard_map/ppermute | solution.py:399
  35.7 1.9 %shard_map.68.sum_ref = f32[2,160,640]{2,1,0:T(8,128)S(1)} custom-call(bf16[32,24,128]{2,1,0:T(8,128)(2,1)S(1)} %all_to_all.5.own_ref), custom_call_target="tpu_custom_call" | custom-call | tf_op jit(solution)/shard_map/pallas_call | solution.py:405
  37.6 2.1 %shard_map.69 = (bf16[9,40,128]{2,1,0:T(8,128)(2,1)S(1)}, bf16[9,40,128]{2,1,0:T(8,128)(2,1)S(1)}, bf16[9,40,128]{2,1,0:T(8,128)(2,1)S(1)}, bf16[9,40,128]{2,1,0:T(8,128)(2,1)S(1)}) custom-call(bf16[32,24,128]{2,1,0:T(8,128)(2,1)S(1)} %collective-permute-done.3.other_ref, f32[2,160,640]{2,1,0:T(8,128)S(1)} %shard_map.68.sum_ref), custom_call_target="tpu_custom_call" | custom-call | tf_op jit(solution)/shard_map/pallas_call | solution.py:410
  39.8 0.4 collective-permute-start.4
  40.2 1.7 %collective-permute-start.5 = (bf16[9,40,128]{2,1,0:T(8,128)(2,1)S(1)}, bf16[9,40,128]{2,1,0:T(8,128)(2,1)S(1)}, u32[]{:S(2)}, u32[]{:S(2)}) collective-permute-start(bf16[9,40,128]{2,1,0:T(8,128)(2,1)S(1)} %get-tuple-element.15), channel_id=1, source_target_pairs={{0,128},{4,132},{8,136},{12,140},{16,144},{20,148},{24,152},{28,15... | collective-permute-start | bytes 276488 | tf_op jit(solution)/shard_map/ppermute | solution.py:417
  41.9 1.2 %collective-permute-start.6 = (bf16[9,40,128]{2,1,0:T(8,128)(2,1)S(1)}, bf16[9,40,128]{2,1,0:T(8,128)(2,1)S(1)}, u32[]{:S(2)}, u32[]{:S(2)}) collective-permute-start(bf16[9,40,128]{2,1,0:T(8,128)(2,1)S(1)} %get-tuple-element.16), channel_id=1, source_target_pairs={{0,192},{4,196},{8,200},{12,204},{16,208},{20,212},{24,216},{28,22... | collective-permute-start | bytes 276488 | tf_op jit(solution)/shard_map/ppermute | solution.py:417
  43.1 4.2 %collective-permute-done.4.one_ref = bf16[9,40,128]{2,1,0:T(8,128)(2,1)S(1)} collective-permute-done((bf16[9,40,128]{2,1,0:T(8,128)(2,1)S(1)}, bf16[9,40,128]{2,1,0:T(8,128)(2,1)S(1)}, u32[]{:S(2)}, u32[]{:S(2)}) %collective-permute-start.4) | collective-permute-done | bytes 92192 | tf_op jit(solution)/shard_map/ppermute | solution.py:417
  47.3 0.3 collective-permute-done.6.three_ref
  47.6 0.9 %shard_map.70 = bf16[34,40,128]{2,1,0:T(8,128)(2,1)} custom-call(bf16[9,40,128]{2,1,0:T(8,128)(2,1)S(1)} %get-tuple-element.13.zero_ref, bf16[9,40,128]{2,1,0:T(8,128)(2,1)S(1)} %collective-permute-done.4.one_ref, bf16[9,40,128]{2,1,0:T(8,128)(2,1)S(1)} %collective-permute-done.5.two_ref, bf16[9,40,128]{2,1,0:T(8,128)(2,1)S(1)} %collective-permute-done.6.three_ref), custom_call_target="tpu_custom_call" | custom-call | tf_op jit(solution)/shard_map/pallas_call | solution.py:418
  (11 shorter events, 0.0 us)
Async XLA Ops:
  0.0 1.7 %copy-start = (bf16[320,3456]{1,0:T(8,128)(2,1)S(1)}, bf16[320,3456]{1,0:T(8,128)(2,1)}, u32[]{:S(2)}) copy-start(bf16[320,3456]{1,0:T(8,128)(2,1)} %jac_ref.1) | copy-start | bytes 6635524
  0.0 0.9 %copy-start.2 = (bf16[320,64]{0,1:T(8,128)(2,1)S(1)}, bf16[320,64]{0,1:T(8,128)(2,1)}, u32[]{:S(2)}) copy-start(bf16[320,64]{0,1:T(8,128)(2,1)} %param.7) | copy-start | bytes 122884
  1.7 7.8 %copy-start.5 = (s32[320]{0:T(512)S(1)}, s32[320]{0:T(512)}, u32[]{:S(2)}) copy-start(s32[320]{0:T(512)} %param.10) | copy-start | bytes 3844
  1.7 7.8 %copy-start.1 = (s32[320,54]{0,1:T(8,128)S(1)}, s32[320,54]{0,1:T(8,128)}, u32[]{:S(2)}) copy-start(s32[320,54]{0,1:T(8,128)} %param.8) | copy-start | bytes 207364
  1.8 7.8 %copy-start.3 = (bf16[320,54]{0,1:T(8,128)(2,1)S(1)}, bf16[320,54]{0,1:T(8,128)(2,1)}, u32[]{:S(2)}) copy-start(bf16[320,54]{0,1:T(8,128)(2,1)} %param.9) | copy-start | bytes 103684
  1.8 7.8 %copy-start.4 = (s32[64]{0:T(128)S(1)}, s32[64]{0:T(128)}, u32[]{:S(2)}) copy-start(s32[64]{0:T(128)} %param.11) | copy-start | bytes 772
  3.1 7.1 %collective-permute-start = (f32[144,128]{1,0:T(8,128)S(1)}, f32[144,128]{1,0:T(8,128)S(1)}, u32[]{:S(2)}, u32[]{:S(2)}) collective-permute-start(f32[144,128]{1,0:T(8,128)S(1)} %shard_map.65.own_ref), channel_id=1, source_target_pairs={{0,2},{1,3},{2,0},{3,1},{4,6},{5,7},{6,4},{7,5},{8,10},{9,11},{10,... | collective-permute-start | bytes 221192 | tf_op jit(solution)/shard_map/ppermute | solution.py:382
  6.9 5.6 %collective-permute-start.1 = (f32[144,128]{1,0:T(8,128)S(1)}, f32[144,128]{1,0:T(8,128)S(1)}, u32[]{:S(2)}, u32[]{:S(2)}) collective-permute-start(f32[144,128]{1,0:T(8,128)S(1)} %shard_map.65.own_ref), channel_id=1, source_target_pairs={{0,1},{1,2},{2,3},{3,0},{4,5},{5,6},{6,7},{7,4},{8,9},{9,10},{10,1... | collective-permute-start | bytes 221192 | tf_op jit(solution)/shard_map/ppermute | solution.py:382
  7.3 5.2 %collective-permute-start.2 = (f32[144,128]{1,0:T(8,128)S(1)}, f32[144,128]{1,0:T(8,128)S(1)}, u32[]{:S(2)}, u32[]{:S(2)}) collective-permute-start(f32[144,128]{1,0:T(8,128)S(1)} %shard_map.65.own_ref), channel_id=1, source_target_pairs={{0,3},{1,0},{2,1},{3,2},{4,7},{5,4},{6,5},{7,6},{8,11},{9,8},{10,9... | collective-permute-start | bytes 221192 | tf_op jit(solution)/shard_map/ppermute | solution.py:382
  31.9 5.7 %collective-permute-start.3 = (bf16[32,24,128]{2,1,0:T(8,128)(2,1)S(1)}, bf16[32,24,128]{2,1,0:T(8,128)(2,1)S(1)}, u32[]{:S(2)}, u32[]{:S(2)}) collective-permute-start(bf16[32,24,128]{2,1,0:T(8,128)(2,1)S(1)} %all_to_all.5.own_ref), channel_id=1, source_target_pairs={{0,4},{4,0},{8,12},{12,8},{16,20},{20,16},{24,28},{28,24},{32,36},... | collective-permute-start | bytes 589832 | tf_op jit(solution)/shard_map/ppermute | solution.py:399
  39.8 7.6 %collective-permute-start.4 = (bf16[9,40,128]{2,1,0:T(8,128)(2,1)S(1)}, bf16[9,40,128]{2,1,0:T(8,128)(2,1)S(1)}, u32[]{:S(2)}, u32[]{:S(2)}) collective-permute-start(bf16[9,40,128]{2,1,0:T(8,128)(2,1)S(1)} %get-tuple-element.14), channel_id=1, source_target_pairs={{0,64},{4,68},{8,72},{12,76},{16,80},{20,84},{24,88},{28,92},{32,9... | collective-permute-start | bytes 276488 | tf_op jit(solution)/shard_map/ppermute | solution.py:417
  40.2 7.1 %collective-permute-start.5 = (bf16[9,40,128]{2,1,0:T(8,128)(2,1)S(1)}, bf16[9,40,128]{2,1,0:T(8,128)(2,1)S(1)}, u32[]{:S(2)}, u32[]{:S(2)}) collective-permute-start(bf16[9,40,128]{2,1,0:T(8,128)(2,1)S(1)} %get-tuple-element.15), channel_id=1, source_target_pairs={{0,128},{4,132},{8,136},{12,140},{16,144},{20,148},{24,152},{28,15... | collective-permute-start | bytes 276488 | tf_op jit(solution)/shard_map/ppermute | solution.py:417
  41.9 5.7 %collective-permute-start.6 = (bf16[9,40,128]{2,1,0:T(8,128)(2,1)S(1)}, bf16[9,40,128]{2,1,0:T(8,128)(2,1)S(1)}, u32[]{:S(2)}, u32[]{:S(2)}) collective-permute-start(bf16[9,40,128]{2,1,0:T(8,128)(2,1)S(1)} %get-tuple-element.16), channel_id=1, source_target_pairs={{0,192},{4,196},{8,200},{12,204},{16,208},{20,212},{24,216},{28,22... | collective-permute-start | bytes 276488 | tf_op jit(solution)/shard_map/ppermute | solution.py:417
